TPU v7x, 512 devices: a whole 4x4x16 slice. The times are simulated.
512 devices in a mesh: row: 32 (over x, y, core), col: 16 (over z).
Axes of the slice: x: 4, y: 4, z: 16, core: 2. Of those that a mesh axis runs over, the one named last changes fastest.
Arguments:
- slip_rate: bfloat16 [128, 32, 128, 256], P('row', 'col'), may hold values from -6 to 6
- near_lists: int32 [128, 32, 6], P('row', 'col'), may hold values from 0 to 8, as said below
- near_blocks: bfloat16 [128, 32, 6, 128, 128], P('row', 'col'), may hold values from -0.21875 to 0.21875
- source_basis: bfloat16 [128, 32, 64, 128], P('row', 'col'), may hold values from -0.5 to 0.5
- target_basis: bfloat16 [128, 32, 64, 128], P('row', 'col'), may hold values from -0.75 to 0.75
- leaf_up: float32 [128, 32, 64, 64], P('row', 'col'), may hold values from -0.25 to 0.25
- leaf_down: float32 [128, 32, 64, 64], P('row', 'col'), may hold values from -0.75 to 0.75
- strip_up: float32 [32, 4, 2, 64, 64], P('row'), may hold values from -0.5 to 0.5
- strip_down: float32 [32, 4, 2, 64, 64], P('row'), may hold values from -0.75 to 0.75
- strip_lists: int32 [32, 16], P('row'), may hold values from 0 to 31, as said below
- coupling: float32 [32, 16, 64, 64], P('row'), may hold values from -0.1875 to 0.1875
Outputs:
- stress_rate: bfloat16 [128, 32, 128, 256], P('row', 'col')
Inputs may be any that keep to these rules, and one draw needn't show every extreme that they name: `near_lists`: entry q names the neighbour leaf at offset (q // 3 - 1, q % 3 - 1); the first entry of every leaf is 4, its own block; the 6 entries of one leaf are distinct. `strip_lists`: strip r lists 16 distinct strips s with |s - r| >= 2.
All inputs are finite; a program needn't handle non-finite values.
Results may differ from a plain program's by a relative error of at most 0.0047.
Values may be sent and summed in bfloat16 or wider, within the bound.
No kernel may reach another device: no remote copies, remote signals or barrier semaphores. Data moves between devices by JAX's collectives and lax.ppermute only.
A program may use at most 64 MiB of HBM per device.

v0:
```python
import jax
import jax.numpy as jnp
from jax import lax
from jax.sharding import PartitionSpec as P


def with_halo(value, sides, width):
    for axis, dim in sides:
        size, length = (lax.axis_size(axis), value.shape[dim])
        up = [(i, (i + 1) % size) for i in range(size - 1)]
        down = [(j, i) for i, j in up]
        last = lax.slice_in_dim(value, length - width, length, axis=dim)
        initial = lax.slice_in_dim(value, 0, width, axis=dim)
        before = lax.ppermute(last, axis, up)
        after = lax.ppermute(initial, axis, down)
        value = jnp.concatenate([before, value, after], axis=dim)
    return value


def from_partner(block, axis, distance):
    count = lax.axis_size(axis)
    route = []
    for low in range(count):
        high = low | 1 << distance
        if high != low and high < count:
            route += [(low, high), (high, low)]
    return lax.ppermute(block, axis, route)


def body(
    slip_rate,
    near_lists,
    near_blocks,
    source_basis,
    target_basis,
    leaf_up,
    leaf_down,
    strip_up,
    strip_down,
    strip_lists,
    coupling,
):
    highest = lax.Precision.HIGHEST
    along_leaves = slip_rate.shape[0]
    dip_leaves = slip_rate.shape[1]
    padded = with_halo(slip_rate, (("row", 0), ("col", 1)), 1)
    views = jnp.stack(
        [
            padded[row_off : row_off + along_leaves, col_off : col_off + dip_leaves]
            for row_off in range(3)
            for col_off in range(3)
        ],
        axis=2,
    )
    chosen = jnp.take_along_axis(views, near_lists[:, :, :, None, None], axis=2)
    near_field = jnp.einsum(
        "abnij,abnje->abie", near_blocks, chosen, preferred_element_type=jnp.float32
    )
    moments = jnp.einsum(
        "abkt,abte->abke", source_basis, slip_rate, preferred_element_type=jnp.float32
    )
    device_moment = jnp.einsum("abkq,abqe->ke", leaf_up, moments, precision=highest)
    col_position = lax.axis_index("col")
    tree_levels = strip_up.shape[1]
    node_moment = device_moment
    for tree_level in range(tree_levels):
        child_side = col_position >> tree_level & 1
        carried = jnp.dot(strip_up[0, tree_level, child_side], node_moment, precision=highest)
        node_moment = carried + from_partner(carried, "col", tree_level)
    strip_entries = strip_lists[0]
    strip_weights = coupling[0]
    fragment = lax.all_gather(node_moment[None], "row", axis=0, tiled=True)
    selector = (
        strip_entries[:, None] == jnp.arange(fragment.shape[0], dtype=jnp.int32)[None, :]
    ).astype(jnp.float32)
    fragment_weights = jnp.einsum("ap,akq->pkq", selector, strip_weights, precision=highest)
    strip_coeff = jnp.einsum("pkq,pqe->ke", fragment_weights, fragment, precision=highest)
    coefficient = strip_coeff
    for tree_level in reversed(range(tree_levels)):
        child_side = col_position >> tree_level & 1
        coefficient = jnp.dot(strip_down[0, tree_level, child_side], coefficient, precision=highest)
    leaf_coeff = jnp.einsum("abkq,qe->abke", leaf_down, coefficient, precision=highest).astype(
        jnp.bfloat16
    )
    far_field = jnp.einsum(
        "abkt,abke->abte", target_basis, leaf_coeff, preferred_element_type=jnp.float32
    )
    return (near_field + far_field).astype(jnp.bfloat16)


def solution(mesh):
    in_specs = (
        P("row", "col", None, None),
        P("row", "col", None),
        P("row", "col", None, None, None),
        P("row", "col", None, None),
        P("row", "col", None, None),
        P("row", "col", None, None),
        P("row", "col", None, None),
        P("row", None, None, None, None),
        P("row", None, None, None, None),
        P("row", None),
        P("row", None, None, None),
    )
    out_specs = P("row", "col", None, None)
    return jax.shard_map(body, mesh=mesh, in_specs=in_specs, out_specs=out_specs, check_vma=False)
```

profile of v0, /device:TPU:1, one launch (start us, length us, event | category | flops | bytes accessed | tf_op | source)
XLA Modules:
  0.0 134.4 jit_solution(15473082735393694711)
XLA Ops:
  6.5 0.0 copy-start
  6.5 0.0 copy-start.6
  6.5 0.0 all-gather.3.cloned.1.call-start
  6.6 1.4 %fusion.79 = f32[4,2,64,256]{3,2,1,0:T(8,128)S(1)} fusion(bf16[4,2,64,128]{3,2,1,0:T(8,128)(2,1)} %param.14, bf16[4,2,128,256]{3,2,1,0:T(8,128)(2,1)} %param.11), kind=kOutput, calls=%fused_computation.102 | convolution fusion | flops 33554432 | bytes 1179648 | tf_op jit(solution)/shard_map/abkt,abte->abke/dot_general | solution.py:59
  8.0 0.0 copy-start.1
  8.0 2.8 %convolution_bitcast_fusion = f32[256,64]{1,0:T(8,128)S(1)} fusion(f32[4,2,64,256]{3,2,1,0:T(8,128)S(1)} %fusion.79, f32[4,2,64,64]{3,2,1,0:T(8,128)} %param.16), kind=kOutput, calls=%fused_computation.19 | convolution fusion | flops 100663296 | bytes 720896 | tf_op jit(solution)/shard_map/abkq,abqe->ke/dot_general | solution.py:62
  10.8 1.0 fusion.39
  11.9 4.4 %collective-permute-start.4 = (f32[64,256]{1,0:T(8,128)S(1)}, f32[64,256]{1,0:T(8,128)S(1)}, u32[]{:S(2)}, u32[]{:S(2)}) collective-permute-start(f32[64,256]{1,0:T(8,128)S(1)} %fusion.39), channel_id=1, source_target_pairs={{0,1},{1,0},{2,3},{3,2},{4,5},{5,4},{6,7},{7,6},{8,9},{9,8},{10,11... | collective-permute-start | bytes 196616 | tf_op jit(solution)/shard_map/ppermute | solution.py:27
  16.3 1.6 %collective-permute-done.4 = f32[64,256]{1,0:T(8,128)S(1)} collective-permute-done((f32[64,256]{1,0:T(8,128)S(1)}, f32[64,256]{1,0:T(8,128)S(1)}, u32[]{:S(2)}, u32[]{:S(2)}) %collective-permute-start.4) | collective-permute-done | bytes 65568 | tf_op jit(solution)/shard_map/ppermute | solution.py:27
  17.9 1.0 fusion.37
  18.9 4.9 %collective-permute-start.5 = (f32[64,256]{1,0:T(8,128)S(1)}, f32[64,256]{1,0:T(8,128)S(1)}, u32[]{:S(2)}, u32[]{:S(2)}) collective-permute-start(f32[64,256]{1,0:T(8,128)S(1)} %fusion.37), channel_id=1, source_target_pairs={{0,2},{2,0},{1,3},{3,1},{4,6},{6,4},{5,7},{7,5},{8,10},{10,8},{9,1... | collective-permute-start | bytes 196616 | tf_op jit(solution)/shard_map/ppermute | solution.py:27
  23.8 1.6 %collective-permute-done.5 = f32[64,256]{1,0:T(8,128)S(1)} collective-permute-done((f32[64,256]{1,0:T(8,128)S(1)}, f32[64,256]{1,0:T(8,128)S(1)}, u32[]{:S(2)}, u32[]{:S(2)}) %collective-permute-start.5) | collective-permute-done | bytes 65568 | tf_op jit(solution)/shard_map/ppermute | solution.py:27
  25.4 1.0 fusion.35
  26.4 8.8 %collective-permute-start.6 = (f32[64,256]{1,0:T(8,128)S(1)}, f32[64,256]{1,0:T(8,128)S(1)}, u32[]{:S(2)}, u32[]{:S(2)}) collective-permute-start(f32[64,256]{1,0:T(8,128)S(1)} %fusion.35), channel_id=1, source_target_pairs={{0,4},{4,0},{1,5},{5,1},{2,6},{6,2},{3,7},{7,3},{8,12},{12,8},{9,1... | collective-permute-start | bytes 196616 | tf_op jit(solution)/shard_map/ppermute | solution.py:27
  35.2 1.6 %collective-permute-done.6 = f32[64,256]{1,0:T(8,128)S(1)} collective-permute-done((f32[64,256]{1,0:T(8,128)S(1)}, f32[64,256]{1,0:T(8,128)S(1)}, u32[]{:S(2)}, u32[]{:S(2)}) %collective-permute-start.6) | collective-permute-done | bytes 65568 | tf_op jit(solution)/shard_map/ppermute | solution.py:27
  36.8 1.0 fusion.33
  37.8 15.7 %collective-permute-start.7 = (f32[64,256]{1,0:T(8,128)S(1)}, f32[64,256]{1,0:T(8,128)S(1)}, u32[]{:S(2)}, u32[]{:S(2)}) collective-permute-start(f32[64,256]{1,0:T(8,128)S(1)} %fusion.33), channel_id=1, source_target_pairs={{0,8},{8,0},{1,9},{9,1},{2,10},{10,2},{3,11},{11,3},{4,12},{12,4},... | collective-permute-start | bytes 196616 | tf_op jit(solution)/shard_map/ppermute | solution.py:27
  53.5 1.6 %collective-permute-done.7 = f32[64,256]{1,0:T(8,128)S(1)} collective-permute-done((f32[64,256]{1,0:T(8,128)S(1)}, f32[64,256]{1,0:T(8,128)S(1)}, u32[]{:S(2)}, u32[]{:S(2)}) %collective-permute-start.7) | collective-permute-done | bytes 65568 | tf_op jit(solution)/shard_map/ppermute | solution.py:27
  55.2 0.6 add.50
  55.8 0.0 all-gather.3.cloned.1.call-update
  55.8 1.0 fusion.78
  56.8 9.4 %collective-permute-start = (bf16[1,2,128,256]{3,2,1,0:T(8,128)(2,1)S(1)}, bf16[1,2,128,256]{3,2,1,0:T(8,128)(2,1)S(1)}, u32[]{:S(2)}, u32[]{:S(2)}) collective-permute-start(bf16[1,2,128,256]{3,2,1,0:T(8,128)(2,1)S(1)} %get-tuple-element.8), channel_id=1, source_target_pairs={{0,16},{16,32},{32,48},{48,64},{64,80},{80,96},{96,112},{112,128},... | collective-permute-start | bytes 393224 | tf_op jit(solution)/shard_map/ppermute | solution.py:14
  66.3 1.9 %collective-permute-start.1 = (bf16[1,2,128,256]{3,2,1,0:T(8,128)(2,1)S(1)}, bf16[1,2,128,256]{3,2,1,0:T(8,128)(2,1)S(1)}, u32[]{:S(2)}, u32[]{:S(2)}) collective-permute-start(bf16[1,2,128,256]{3,2,1,0:T(8,128)(2,1)S(1)} %get-tuple-element.7), channel_id=1, source_target_pairs={{16,0},{32,16},{48,32},{64,48},{80,64},{96,80},{112,96},{128,112},... | collective-permute-start | bytes 393224 | tf_op jit(solution)/shard_map/ppermute | solution.py:15
  68.2 0.7 bitcast_or_fusion
  68.9 0.1 reshape.22
  69.0 0.0 collective-permute-done
  69.0 1.1 constant_dynamic-update-slice_fusion.1
  70.1 2.5 %collective-permute-done.1 = bf16[1,2,128,256]{3,2,1,0:T(8,128)(2,1)S(1)} collective-permute-done((bf16[1,2,128,256]{3,2,1,0:T(8,128)(2,1)S(1)}, bf16[1,2,128,256]{3,2,1,0:T(8,128)(2,1)S(1)}, u32[]{:S(2)}, u32[]{:S(2)}) %collective-permute-start.1) | collective-permute-done | bytes 131104 | tf_op jit(solution)/shard_map/ppermute | solution.py:15
  72.6 0.1 fusion.77
  72.6 1.3 collective-permute-start.2
  73.9 0.0 copy-done.7
  74.0 1.9 %fusion.31 = f32[32,64,64]{2,0,1:T(8,128)S(1)} fusion(f32[16,64,64]{2,1,0:T(8,128)} %bitcast.103, s32[16]{0:T(128)S(1)} %bitcast.104), kind=kOutput, calls=%fused_computation.48 | convolution fusion | flops 25166336 | bytes 786496 | tf_op jit(solution)/shard_map/ap,akq->pkq/dot_general | solution.py:76
  75.9 1.3 collective-permute-start.3
  77.2 0.0 copy-done.6
  77.2 2.8 %collective-permute-done.2 = bf16[6,1,128,256]{3,2,1,0:T(8,128)(2,1)S(1)} collective-permute-done((bf16[6,1,128,256]{3,2,1,0:T(8,128)(2,1)S(1)}, bf16[6,1,128,256]{3,2,1,0:T(8,128)(2,1)S(1)}, u32[]{:S(2)}, u32[]{:S(2)}) %collective-permute-start.2) | collective-permute-done | bytes 393248 | tf_op jit(solution)/shard_map/ppermute | solution.py:14
  80.0 0.8 fusion.22
  80.8 0.0 copy-done.1
  80.8 0.8 fusion.30
  81.7 4.8 %collective-permute-done.3 = bf16[6,1,128,256]{3,2,1,0:T(8,128)(2,1)S(1)} collective-permute-done((bf16[6,1,128,256]{3,2,1,0:T(8,128)(2,1)S(1)}, bf16[6,1,128,256]{3,2,1,0:T(8,128)(2,1)S(1)}, u32[]{:S(2)}, u32[]{:S(2)}) %collective-permute-start.3) | collective-permute-done | bytes 393248 | tf_op jit(solution)/shard_map/ppermute | solution.py:15
  86.4 0.8 fusion.16
  87.3 0.9 fusion.19
  88.1 0.8 bitcast_dynamic-update-slice_fusion
  89.0 0.8 fusion.13
  89.8 0.8 fusion.28
  90.6 0.8 fusion.26
  91.4 0.8 fusion.24
  92.3 5.0 %gather_fusion = bf16[48,128,256]{2,1,0:T(8,128)(2,1)} fusion(bf16[4,2,9,128,256]{4,3,1,0,2:T(8,128)(2,1)} %fusion.24, s32[48]{0:T(128)S(1)} %reshape.22), kind=kCustom, calls=%fused_computation | custom fusion | bytes 6292032 | tf_op jit(solution)/shard_map/jit(take_along_axis)/gather | solution.py:55
  97.2 4.6 %copy.12 = bf16[4,2,6,128,256]{3,4,2,1,0:T(8,128)(2,1)} copy(bf16[4,2,6,128,256]{4,3,2,1,0:T(8,128)(2,1)} %bitcast.101) | data formatting | bytes 6291456 | tf_op jit(solution)/shard_map/jit(take_along_axis)/gather | solution.py:55
  101.9 0.0 copy-done
  101.9 0.0 copy-start.4
  101.9 4.0 %fusion.4 = f32[4,2,256,128]{3,2,1,0:T(8,128)} fusion(bf16[4,2,6,128,128]{4,3,2,1,0:T(8,128)(2,1)S(1)} %copy-done, bf16[4,2,6,128,256]{3,4,2,1,0:T(8,128)(2,1)} %copy.12, pred[4,2,6]{2,1,0:T(4,128)(4,1)S(1)} %compare_and_fusion), kind=kOutput, calls=%fused_computation.9 | convolution fusion | flops 404226048 | bytes 5767216 | tf_op jit(solution)/shard_map/abnij,abnje->abie/dot_general | solution.py:56
  105.9 15.5 %all-gather.3.cloned.1.call-done = f32[2048,256]{1,0:T(8,128)} async-done(((f32[64,256]{1,0:T(8,128)}), f32[2048,256]{1,0:T(8,128)}) %all-gather.3.cloned.1.call-update) | async-done | bytes 2097168 | tf_op jit(solution)/shard_map/all_gather | solution.py:72
  121.4 3.4 %convolution_bitcast_fusion.2 = f32[64,256]{1,0:T(8,128)S(1)} fusion(f32[32,64,256]{2,1,0:T(8,128)} %bitcast.102, f32[32,64,64]{2,0,1:T(8,128)S(1)} %fusion.31), kind=kOutput, calls=%fused_computation.21 | convolution fusion | flops 402653184 | bytes 2686976 | tf_op jit(solution)/shard_map/pkq,pqe->ke/dot_general | solution.py:77
  124.7 0.0 copy-done.5
  124.8 0.2 fusion.44
  125.0 0.2 fusion.46
  125.2 0.2 fusion.48
  125.4 0.2 convolution_bitcast_fusion.1
  125.6 0.0 copy-done.3
  125.6 0.6 fusion.9
  126.2 0.0 copy-done.4
  126.2 0.0 copy-done.2
  126.2 0.4 fusion.8
  126.5 1.0 copy.13
  (7 shorter events, 0.0 us)
Async XLA Ops:
  6.5 95.4 %copy-start = (bf16[4,2,6,128,128]{4,3,2,1,0:T(8,128)(2,1)S(1)}, bf16[4,2,6,128,128]{4,3,2,1,0:T(8,128)(2,1)}, u32[]{:S(2)}) copy-start(bf16[4,2,6,128,128]{4,3,2,1,0:T(8,128)(2,1)} %param.13) | copy-start | bytes 4718596
  6.5 70.6 %copy-start.6 = (s32[4,2,6]{2,1,0:T(2,128)S(1)}, s32[4,2,6]{2,1,0:T(2,128)}, u32[]{:S(2)}) copy-start(s32[4,2,6]{2,1,0:T(2,128)} %param.12) | copy-start | bytes 580
  6.5 67.4 %copy-start.7 = (s32[1,16]{1,0:T(1,128)S(1)}, s32[1,16]{1,0:T(1,128)}, u32[]{:S(2)}) copy-start(s32[1,16]{1,0:T(1,128)} %param.20) | copy-start | bytes 196
  6.5 114.8 %all-gather.3.cloned.1.call-start = ((), (), s32[]{:S(2)}) async-start(), calls=%async_computation | async-start | bytes 2162688 | tf_op jit(solution)/shard_map/all_gather | solution.py:72
  8.0 72.8 %copy-start.1 = (bf16[4,2,128,256]{3,2,1,0:T(8,128)(2,1)S(1)}, bf16[4,2,128,256]{3,2,1,0:T(8,128)(2,1)}, u32[]{:S(2)}) copy-start(bf16[4,2,128,256]{3,2,1,0:T(8,128)(2,1)} %param.11) | copy-start | bytes 1572868
  11.9 6.0 %collective-permute-start.4 = (f32[64,256]{1,0:T(8,128)S(1)}, f32[64,256]{1,0:T(8,128)S(1)}, u32[]{:S(2)}, u32[]{:S(2)}) collective-permute-start(f32[64,256]{1,0:T(8,128)S(1)} %fusion.39), channel_id=1, source_target_pairs={{0,1},{1,0},{2,3},{3,2},{4,5},{5,4},{6,7},{7,6},{8,9},{9,8},{10,11... | collective-permute-start | bytes 196616 | tf_op jit(solution)/shard_map/ppermute | solution.py:27
  18.9 6.5 %collective-permute-start.5 = (f32[64,256]{1,0:T(8,128)S(1)}, f32[64,256]{1,0:T(8,128)S(1)}, u32[]{:S(2)}, u32[]{:S(2)}) collective-permute-start(f32[64,256]{1,0:T(8,128)S(1)} %fusion.37), channel_id=1, source_target_pairs={{0,2},{2,0},{1,3},{3,1},{4,6},{6,4},{5,7},{7,5},{8,10},{10,8},{9,1... | collective-permute-start | bytes 196616 | tf_op jit(solution)/shard_map/ppermute | solution.py:27
  26.4 10.5 %collective-permute-start.6 = (f32[64,256]{1,0:T(8,128)S(1)}, f32[64,256]{1,0:T(8,128)S(1)}, u32[]{:S(2)}, u32[]{:S(2)}) collective-permute-start(f32[64,256]{1,0:T(8,128)S(1)} %fusion.35), channel_id=1, source_target_pairs={{0,4},{4,0},{1,5},{5,1},{2,6},{6,2},{3,7},{7,3},{8,12},{12,8},{9,1... | collective-permute-start | bytes 196616 | tf_op jit(solution)/shard_map/ppermute | solution.py:27
  37.8 17.4 %collective-permute-start.7 = (f32[64,256]{1,0:T(8,128)S(1)}, f32[64,256]{1,0:T(8,128)S(1)}, u32[]{:S(2)}, u32[]{:S(2)}) collective-permute-start(f32[64,256]{1,0:T(8,128)S(1)} %fusion.33), channel_id=1, source_target_pairs={{0,8},{8,0},{1,9},{9,1},{2,10},{10,2},{3,11},{11,3},{4,12},{12,4},... | collective-permute-start | bytes 196616 | tf_op jit(solution)/shard_map/ppermute | solution.py:27
  56.8 12.2 %collective-permute-start = (bf16[1,2,128,256]{3,2,1,0:T(8,128)(2,1)S(1)}, bf16[1,2,128,256]{3,2,1,0:T(8,128)(2,1)S(1)}, u32[]{:S(2)}, u32[]{:S(2)}) collective-permute-start(bf16[1,2,128,256]{3,2,1,0:T(8,128)(2,1)S(1)} %get-tuple-element.8), channel_id=1, source_target_pairs={{0,16},{16,32},{32,48},{48,64},{64,80},{80,96},{96,112},{112,128},... | collective-permute-start | bytes 393224 | tf_op jit(solution)/shard_map/ppermute | solution.py:14
  66.3 6.3 %collective-permute-start.1 = (bf16[1,2,128,256]{3,2,1,0:T(8,128)(2,1)S(1)}, bf16[1,2,128,256]{3,2,1,0:T(8,128)(2,1)S(1)}, u32[]{:S(2)}, u32[]{:S(2)}) collective-permute-start(bf16[1,2,128,256]{3,2,1,0:T(8,128)(2,1)S(1)} %get-tuple-element.7), channel_id=1, source_target_pairs={{16,0},{32,16},{48,32},{64,48},{80,64},{96,80},{112,96},{128,112},... | collective-permute-start | bytes 393224 | tf_op jit(solution)/shard_map/ppermute | solution.py:15
  72.6 7.4 %collective-permute-start.2 = (bf16[6,1,128,256]{3,2,1,0:T(8,128)(2,1)S(1)}, bf16[6,1,128,256]{3,2,1,0:T(8,128)(2,1)S(1)}, u32[]{:S(2)}, u32[]{:S(2)}) collective-permute-start(bf16[6,1,128,256]{3,2,1,0:T(8,128)(2,1)S(1)} %get-tuple-element.6), channel_id=1, source_target_pairs={{0,1},{1,2},{2,3},{3,4},{4,5},{5,6},{6,7},{7,8},{8,9},{9,10},{10,1... | collective-permute-start | bytes 1179656 | tf_op jit(solution)/shard_map/ppermute | solution.py:14
  75.9 10.6 %collective-permute-start.3 = (bf16[6,1,128,256]{3,2,1,0:T(8,128)(2,1)S(1)}, bf16[6,1,128,256]{3,2,1,0:T(8,128)(2,1)S(1)}, u32[]{:S(2)}, u32[]{:S(2)}) collective-permute-start(bf16[6,1,128,256]{3,2,1,0:T(8,128)(2,1)S(1)} %get-tuple-element.5), channel_id=1, source_target_pairs={{1,0},{2,1},{3,2},{4,3},{5,4},{6,5},{7,6},{8,7},{9,8},{10,9},{11,1... | collective-permute-start | bytes 1179656 | tf_op jit(solution)/shard_map/ppermute | solution.py:15
  101.9 22.9 %copy-start.5 = (f32[1,4,2,64,64]{4,3,2,1,0:T(8,128)S(1)}, f32[1,4,2,64,64]{4,3,2,1,0:T(8,128)}, u32[]{:S(2)}) copy-start(f32[1,4,2,64,64]{4,3,2,1,0:T(8,128)} %param.19) | copy-start | bytes 393220
  101.9 23.7 %copy-start.3 = (f32[4,2,64,64]{3,2,1,0:T(8,128)S(1)}, f32[4,2,64,64]{3,2,1,0:T(8,128)}, u32[]{:S(2)}) copy-start(f32[4,2,64,64]{3,2,1,0:T(8,128)} %param.17) | copy-start | bytes 393220
  101.9 24.3 %copy-start.4 = (bf16[4,2,64,128]{3,2,1,0:T(8,128)(2,1)S(1)}, bf16[4,2,64,128]{3,2,1,0:T(8,128)(2,1)}, u32[]{:S(2)}) copy-start(bf16[4,2,64,128]{3,2,1,0:T(8,128)(2,1)} %param.15) | copy-start | bytes 393220
  121.4 4.8 %copy-start.2 = (f32[4,2,256,128]{3,2,1,0:T(8,128)S(1)}, f32[4,2,256,128]{3,2,1,0:T(8,128)}, u32[]{:S(2)}) copy-start(f32[4,2,256,128]{3,2,1,0:T(8,128)} %fusion.4) | copy-start | bytes 3145732
Sparse Core Ops, SparseCore 0:
  56.0 65.3 all-gather.2
where the time goes:
time: 135 us; the launch traced here: 134 us
  starting transfers between devices  47.8 us (35%)
  waiting for transfers between devices  32.1 us (24%)
  matrix products  19.1 us (14%)
  local copies, waits for them, and re-layouts  13.7 us (10%)
  between operations  13.7 us (10%)
  other arithmetic  8.03 us (6%)
    ppermute x4, starting transfers between devices, from_partner(): return lax.ppermute(block, axis, route)  33.8 us
    all_gather x1, waiting for transfers between devices, body(): fragment = lax.all_gather(node_moment[None], 'row', axis=0, tiled=True)  15.5 us
    ppermute x2, starting transfers between devices, with_halo(): before = lax.ppermute(last, axis, up)  10.7 us
    gather x3, local copies, waits for them, and re-layouts, body(): chosen = jnp.take_along_axis(views, near_lists[:, :, :, None, None], axis=2)  9.69 us
    ppermute x2, waiting for transfers between devices, with_halo(): after = lax.ppermute(initial, axis, down)  7.24 us
    ppermute x4, waiting for transfers between devices, from_partner(): return lax.ppermute(block, axis, route)  6.55 us
    unnamed x7, other arithmetic  5.84 us
    dot_general x1, matrix products, body(): jnp.einsum('abnij,abnje->abie', near_blocks, chosen, preferred_element_ty...  3.97 us
  transfers between devices with their start and end apart: 9, of which 8 were waited for; matrix products, arithmetic and copies ran while one was open for 19% of the time, Pallas kernels for 0%

commit v1 on v0

v1 whole, which is shorter than its diff:
```python
import jax
import jax.numpy as jnp
from jax import lax
from jax.experimental import pallas as pl
from jax.experimental.pallas import tpu as pltpu
from jax.sharding import PartitionSpec as P

F32 = jnp.float32
BF16 = jnp.bfloat16
QUARTERS = 4


def halves(value):
    high = value.astype(BF16)
    return high, (value - high.astype(F32)).astype(BF16)


def dot(left, right):
    return jnp.dot(left, right, preferred_element_type=F32)


def dot_split(left, right):
    rows = left.shape[0]
    left_high, left_low = halves(left)
    right_high, right_low = halves(right)
    both = dot(jnp.concatenate([left_high, left_low], axis=0), right_high)
    return both[:rows] + both[rows:] + dot(left_high, right_low)


def chain_of(ref, col, levels):
    return [ref[level, (col >> level) & 1] for level in range(levels)]


def pack(tile, odd):
    half = tile.shape[0] // 2
    lane = lax.broadcasted_iota(jnp.int32, (half, tile.shape[1]), 1)
    left = lane < tile.shape[1] // 2
    upper, lower = tile[:half], tile[half:]
    shift = tile.shape[1] // 2
    if odd:
        return jnp.where(left, pltpu.roll(upper, shift, 1), lower)
    return jnp.where(left, upper, pltpu.roll(lower, shift, 1))


def fetch(refs, buffers, sems):
    copies = [
        pltpu.make_async_copy(ref, buffer, sems.at[at])
        for at, (ref, buffer) in enumerate(zip(refs, buffers, strict=True))
    ]
    for copy in copies:
        copy.start()
    return copies


def up_kernel(
    strip_up_ref, leaf_up_ref, basis_ref, slip_ref, out_ref, strip_up, leaf_up, basis, slip, sems
):
    leaves = slip_ref.shape[0]
    copies = fetch(
        (strip_up_ref, leaf_up_ref, basis_ref, slip_ref), (strip_up, leaf_up, basis, slip), sems
    )
    copies[0].wait()
    s0, s1, s2, s3 = chain_of(strip_up, lax.axis_index("col"), 4)
    chain = dot_split(dot_split(s3, s2), dot_split(s1, s0))
    copies[1].wait()
    ups = jnp.concatenate([leaf_up[leaf] for leaf in range(leaves)], axis=1)
    copies[2].wait()
    copies[3].wait()
    moments = jnp.concatenate([dot(basis[leaf], slip[leaf]) for leaf in range(leaves)], axis=0)
    node = dot_split(chain, dot_split(ups, moments))
    for quarter in range(QUARTERS):
        half = quarter // 2
        packed = pack(node[:, 128 * half : 128 * (half + 1)], quarter % 2).astype(BF16)
        for copy in range(out_ref.shape[0] // QUARTERS):
            out_ref[copy * QUARTERS + quarter] = packed


def sum_kernel(in_ref, before_ref, after_ref, out_ref):
    del before_ref, after_ref
    total = jnp.sum(in_ref[...].astype(F32), axis=0).astype(BF16)
    for copy in range(out_ref.shape[0]):
        out_ref[copy] = total


def weights_kernel(lists_ref, coupling_ref, after_ref, out_ref, coupling, wide, sems):
    del after_ref
    (copy,) = fetch((coupling_ref,), (coupling,), sems)
    strips, rank = coupling.shape[0], coupling.shape[1]
    half = rank // 2
    columns = out_ref.shape[1]
    row = lax.broadcasted_iota(jnp.int32, (half, columns), 0)
    column = lax.broadcasted_iota(jnp.int32, (half, columns), 1)
    chosen = [
        jnp.where(column == row + lists_ref[strip] * half, 1.0, 0.0).astype(BF16) for strip in range(strips)
    ]
    copy.wait()
    for strip in range(strips):
        at = slice(strip * half, (strip + 1) * half)
        wide[0:rank, at] = coupling[strip, :, 0:half]
        wide[rank : 2 * rank, at] = coupling[strip, :, half:rank]
    high, low = halves(wide[...])
    both = dot(jnp.concatenate([high, low], axis=0), jnp.concatenate(chosen, axis=0))
    out_ref[...] = both.astype(BF16)


def far_kernel(strip_down_ref, leaf_down_ref, target_ref, after_ref, out_ref, strip_down, leaf_down, target, sems):
    del after_ref
    for copy in fetch((strip_down_ref, leaf_down_ref, target_ref), (strip_down, leaf_down, target), sems):
        copy.wait()
    s0, s1, s2, s3 = chain_of(strip_down, lax.axis_index("col"), 4)
    chain = dot_split(dot_split(s0, s1), dot_split(s2, s3))
    leaves, rank, size = target.shape
    for leaf in range(leaves):
        down_high, down_low = halves(dot_split(leaf_down[leaf], chain))
        turned = target[leaf].astype(F32).T.astype(BF16)
        high, low = halves(dot(turned, down_high) + dot(turned, down_low))
        out_ref[leaf * size : (leaf + 1) * size, 0:rank] = high
        out_ref[leaf * size : (leaf + 1) * size, rank : 2 * rank] = low


def hold_kernel(blocks_ref, after_ref, out_ref, sems):
    del after_ref
    for copy in fetch((blocks_ref,), (out_ref,), sems):
        copy.wait()


def couple_kernel(tops_ref, weights_ref, out_ref):
    rank = weights_ref.shape[0] // 4
    half = rank // 2
    tops = tops_ref[...].reshape(tops_ref.shape[0] * tops_ref.shape[1], tops_ref.shape[2])
    product = dot(weights_ref[...], tops)
    product = product[: 2 * rank] + product[2 * rank :]
    upper, lower = product[:rank], product[rank:]
    lanes = product.shape[1]
    left = lax.broadcasted_iota(jnp.int32, (half, lanes), 1) < lanes // 2
    packed = jnp.where(
        left,
        upper[:half] + pltpu.roll(lower[:half], lanes // 2, 1),
        pltpu.roll(upper[half:], lanes // 2, 1) + lower[half:],
    ).astype(BF16)
    for copy in range(out_ref.shape[0]):
        out_ref[copy] = packed


def rim_kernel(slip_ref, before_ref, after_ref, after_sum_ref, left_ref, right_ref):
    del after_sum_ref
    along, dip = slip_ref.shape[0], slip_ref.shape[1]
    for ref, col in ((left_ref, 0), (right_ref, dip - 1)):
        ref[0] = before_ref[col]
        ref[along + 1] = after_ref[col]
        for row in range(along):
            ref[row + 1] = slip_ref[row, col]


def near_kernel(lists_ref, slip_ref, before_ref, after_ref, left_ref, right_ref, blocks_ref, out_ref, padded):
    along, dip, near = blocks_ref.shape[0], blocks_ref.shape[1], blocks_ref.shape[2]
    width = dip + 2
    for row in range(along + 2):
        padded[row * width] = left_ref[row]
        padded[row * width + width - 1] = right_ref[row]
    for col in range(dip):
        padded[1 + col] = before_ref[col]
        padded[(along + 1) * width + 1 + col] = after_ref[col]
        for row in range(along):
            padded[(row + 1) * width + 1 + col] = slip_ref[row, col]
    for row in range(along):
        for col in range(dip):
            leaf = row * dip + col
            sources = []
            for at in range(near):
                place = lists_ref[leaf * near + at]
                sources.append(padded[(row + place // 3) * width + col + place % 3])
            out_ref[leaf] = dot(
                jnp.concatenate([blocks_ref[row, col, at] for at in range(near)], axis=1),
                jnp.concatenate(sources, axis=0),
            )


def final_kernel(near_ref, far_ref, coeff_ref, out_ref, held, sems):
    leaves, size = held.shape[0], held.shape[1]
    rows, lanes = coeff_ref.shape[1], coeff_ref.shape[2]
    left = lax.broadcasted_iota(jnp.int32, (rows, lanes), 1) < lanes // 2
    tiles = []
    for half in range(2):
        one = coeff_ref[2 * half].astype(F32)
        two = coeff_ref[2 * half + 1].astype(F32)
        upper = jnp.where(left, one, pltpu.roll(two, lanes // 2, 1))
        lower = jnp.where(left, pltpu.roll(one, lanes // 2, 1), two)
        tiles.append(jnp.concatenate([upper, lower], axis=0).astype(BF16))
    coeff = jnp.concatenate(tiles, axis=1)
    coeff = jnp.concatenate([coeff, coeff], axis=0)
    copies = []
    for leaf in range(leaves):
        far = dot(far_ref[leaf * size : (leaf + 1) * size], coeff)
        held[leaf] = (near_ref[leaf] + far).astype(BF16)
        copy = pltpu.make_async_copy(held.at[leaf], out_ref.at[leaf], sems.at[leaf])
        copy.start()
        copies.append(copy)
    for copy in copies:
        copy.wait()


def call(kernel, outs, places, *args, to="v", scratch=(), name=None, flops=0, size=0):
    args = [pltpu.with_memory_space_constraint(a, pltpu.HBM) if p == "h" else a for p, a in zip(places, args, strict=True)]
    spaces = {"s": pltpu.SMEM, "v": pltpu.VMEM, "a": pl.ANY, "h": pltpu.HBM}
    return pl.pallas_call(
        kernel,
        out_shape=outs,
        in_specs=[pl.BlockSpec(memory_space=spaces[p]) for p in places],
        out_specs=jax.tree.map(lambda _: pl.BlockSpec(memory_space=spaces[to]), outs),
        scratch_shapes=scratch,
        compiler_params=pltpu.CompilerParams(vmem_limit_bytes=12 * 1024 * 1024),
        cost_estimate=pl.CostEstimate(flops=flops, bytes_accessed=size, transcendentals=0),
        name=name,
    )(*args)


def body(
    slip_rate,
    near_lists,
    near_blocks,
    source_basis,
    target_basis,
    leaf_up,
    leaf_down,
    strip_up,
    strip_down,
    strip_lists,
    coupling,
):
    along, dip, size, members = slip_rate.shape
    rank = source_basis.shape[2]
    leaves = along * dip
    n_row, n_col = lax.axis_size("row"), lax.axis_size("col")
    sds = jax.ShapeDtypeStruct
    slips = slip_rate.reshape(leaves, size, members)
    piece = (rank // 2, 128)

    dma = pltpu.SemaphoreType.DMA
    mega = 1024 * 1024
    basis = source_basis.reshape(leaves, rank, size)
    target = target_basis.reshape(leaves, rank, size)
    ups = leaf_up.reshape(leaves, rank, rank)
    downs = leaf_down.reshape(leaves, rank, rank)
    couplings = coupling[0]
    strips = couplings.shape[0]

    def room(value):
        return pltpu.VMEM(value.shape, value.dtype)

    parts = call(
        up_kernel,
        sds((n_col, *piece), BF16),
        "hhhh",
        strip_up[0],
        ups,
        basis,
        slips,
        scratch=[room(strip_up[0]), room(ups), room(basis), room(slips), dma((4,))],
        name="up",
        flops=100_000_000,
        size=2 * mega,
    )
    weights = call(
        weights_kernel,
        sds((4 * rank, n_row * rank // 2), BF16),
        "sha",
        strip_lists[0],
        couplings,
        parts,
        scratch=[room(couplings), pltpu.VMEM((2 * rank, strips * rank // 2), F32), dma((1,))],
        name="weights",
        flops=100_000_000,
        size=mega,
    )
    far = call(
        far_kernel,
        sds((leaves * size, 2 * rank), BF16),
        "hhha",
        strip_down[0],
        downs,
        target,
        parts,
        scratch=[room(strip_down[0]), room(downs), room(target), dma((3,))],
        name="far",
        flops=100_000_000,
        size=mega,
    )
    blocks = call(
        hold_kernel,
        sds(near_blocks.shape, BF16),
        "ha",
        near_blocks,
        parts,
        scratch=[dma((1,))],
        name="hold",
        flops=1_000_000,
        size=2 * mega,
    )
    held, _ = lax.optimization_barrier((slip_rate, weights))
    up_row = [(i, i + 1) for i in range(n_row - 1)]
    down_row = [(j, i) for i, j in up_row]
    up_col = [(i, i + 1) for i in range(n_col - 1)]
    down_col = [(j, i) for i, j in up_col]

    parts = lax.all_to_all(parts, "col", 0, 0, tiled=True)
    before = lax.ppermute(held[along - 1], "row", up_row)
    after = lax.ppermute(held[0], "row", down_row)
    tops = call(sum_kernel, sds((n_row, *piece), BF16), "vaa", parts, before, after, name="sum", flops=10_000_000, size=mega // 2)
    rim_left, rim_right = call(
        rim_kernel,
        (sds((along + 2, size, members), BF16), sds((along + 2, size, members), BF16)),
        "vvva",
        held,
        before,
        after,
        tops,
        name="rim",
        flops=1_000_000,
        size=mega,
    )
    tops = lax.all_to_all(tops, "row", 0, 0, tiled=True)
    from_left = lax.ppermute(rim_right, "col", up_col)
    from_right = lax.ppermute(rim_left, "col", down_col)
    coeff = call(
        couple_kernel,
        sds((QUARTERS, *piece), BF16),
        "vv",
        tops,
        weights,
        name="couple",
        flops=30_000_000_000,
        size=mega // 2,
    )
    groups = [list(range(i, i + QUARTERS)) for i in range(0, n_col, QUARTERS)]
    coeff = lax.all_to_all(coeff, "col", 0, 0, tiled=True, axis_index_groups=groups)
    near = call(
        near_kernel,
        sds((leaves, size, members), F32),
        "svvvvvv",
        near_lists.reshape(-1),
        held,
        before,
        after,
        from_left,
        from_right,
        blocks,
        scratch=[pltpu.VMEM(((along + 2) * (dip + 2), size, members), BF16)],
        name="near",
        flops=2 * leaves * 6 * size * size * members,
        size=4 * mega,
    )
    stress = call(
        final_kernel,
        sds((leaves, size, members), BF16),
        "vvv",
        near,
        far,
        coeff,
        to="a",
        scratch=[pltpu.VMEM((leaves, size, members), BF16), dma((leaves,))],
        name="final",
        flops=2 * leaves * size * members * rank * 2,
        size=2 * mega,
    )
    return stress.reshape(along, dip, size, members)


def solution(mesh):
    in_specs = (
        P("row", "col", None, None),
        P("row", "col", None),
        P("row", "col", None, None, None),
        P("row", "col", None, None),
        P("row", "col", None, None),
        P("row", "col", None, None),
        P("row", "col", None, None),
        P("row", None, None, None, None),
        P("row", None, None, None, None),
        P("row", None),
        P("row", None, None, None),
    )
    out_specs = P("row", "col", None, None)
    return jax.shard_map(body, mesh=mesh, in_specs=in_specs, out_specs=out_specs, check_vma=False)
```

time: 135 us -> 62.1 us (0.46)
  waiting for transfers between devices: 32.1 us -> 8.25 us
  matrix products: 19.1 us -> 0 us
  local copies, waits for them, and re-layouts: 13.7 us -> 0.12 us
  between operations: 13.7 us -> 0.17 us
  Pallas kernels: 0 us -> 12.9 us
  other arithmetic: 8.03 us -> 0 us
  starting transfers between devices: 47.8 us -> 40.1 us
    ppermute x8 -> x4, starting transfers between devices: 47.8 us -> 10.4 us  [the longest x1 3.1 us: body(): from_left = lax.ppermute(rim_right, 'col', up_col)]
    all_to_all x0 -> x3, starting transfers between devices: none -> 29.8 us  [the longest x1 15.8 us: body(): parts = lax.all_to_all(parts, 'col', 0, 0, tiled=True)]
    dot_general x15 -> x0, matrix products: 19.1 us -> none  [the longest x1 3.97 us: body(): jnp.einsum('abnij,abnje->abie', near_blocks, chosen, preferred_element_ty...]
    all_gather x1 -> x0, waiting for transfers between devices: 15.5 us -> none  [body(): fragment = lax.all_gather(node_moment[None], 'row', axis=0, tiled=True)]
    ppermute x8 -> x4, waiting for transfers between devices: 16.6 us -> 1.93 us  [the longest x1 1 us: body(): after = lax.ppermute(held[0], 'row', down_row)]
    pallas_call x0 -> x9, Pallas kernels: none -> 12.9 us  [call(): pl.pallas_call(kernel, out_shape=outs, in_specs=[pl.BlockSpec(memory_spac...]
    gather x3 -> x0, local copies, waits for them, and re-layouts: 9.69 us -> none  [body(): chosen = jnp.take_along_axis(views, near_lists[:, :, :, None, None], axis=2)]
    all_to_all x0 -> x3, waiting for transfers between devices: none -> 6.32 us  [the longest x1 4.5 us: body(): tops = lax.all_to_all(tops, 'row', 0, 0, tiled=True)]
  transfers between devices with their start and end apart: 9 -> 7, of which waited for: 8 -> 4; matrix products, arithmetic and copies ran while one was open for 19% -> 0% of each run, Pallas kernels for 0% -> 13%
where the time goes in v1:
time: 62.1 us; the launch traced here: 61.5 us
  starting transfers between devices  40.1 us (65%)
  Pallas kernels  12.9 us (21%)
  waiting for transfers between devices  8.25 us (13%)
    all_to_all x1, starting transfers between devices, body(): parts = lax.all_to_all(parts, 'col', 0, 0, tiled=True)  15.8 us
    pallas_call x9, Pallas kernels, call(): pl.pallas_call(kernel, out_shape=outs, in_specs=[pl.BlockSpec(memory_spac...  12.9 us
    all_to_all x1, starting transfers between devices, body(): tops = lax.all_to_all(tops, 'row', 0, 0, tiled=True)  10.7 us
    all_to_all x1, waiting for transfers between devices, body(): tops = lax.all_to_all(tops, 'row', 0, 0, tiled=True)  4.5 us
    all_to_all x1, starting transfers between devices, body(): lax.all_to_all(coeff, 'col', 0, 0, tiled=True, axis_index_groups=groups)  3.26 us
    ppermute x1, starting transfers between devices, body(): from_left = lax.ppermute(rim_right, 'col', up_col)  3.1 us
    ppermute x1, starting transfers between devices, body(): before = lax.ppermute(held[along - 1], 'row', up_row)  3.1 us
    ppermute x1, starting transfers between devices, body(): after = lax.ppermute(held[0], 'row', down_row)  2.86 us
  transfers between devices with their start and end apart: 7, of which 4 were waited for; matrix products, arithmetic and copies ran while one was open for 0% of the time, Pallas kernels for 13%

profile of v1, /device:TPU:1, one launch (start us, length us, event | category | flops | bytes accessed | tf_op | source)
XLA Modules:
  0.0 61.5 jit_solution(436581418768561463)
XLA Ops:
  0.0 0.0 copy-start
  0.0 0.0 copy-start.1
  0.0 2.8 %up.1.after_ref = bf16[16,32,128]{2,1,0:T(8,128)(2,1)} custom-call(f32[4,2,64,64]{3,2,1,0:T(8,128)} %bitcast.17, f32[8,64,64]{2,1,0:T(8,128)} %bitcast.18, bf16[8,64,128]{2,1,0:T(8,128)(2,1)} %bitcast.21, bf16[8,128,256]{2,1,0:T(8,128)(2,1)} %bitcast.14), custom_call_target="tpu_custom_call" | custom-call | flops 100000000 | bytes 2097152 | tf_op jit(solution)/shard_map/up/pallas_call | solution.py:206
  2.8 15.8 %all-to-all-start = ((bf16[16,32,128]{2,1,0:T(8,128)(2,1)}), bf16[16,32,128]{2,1,0:T(8,128)(2,1)S(1)}, u32[]{:S(2)}, u32[]{:S(2)}) async-start(bf16[16,32,128]{2,1,0:T(8,128)(2,1)} %up.1.after_ref), calls=%async_computation | async-start | bytes 262144 | tf_op jit(solution)/shard_map/all_to_all | solution.py:306
  18.5 0.0 copy-done.1
  18.6 2.2 %weights.1.weights_ref = bf16[256,1024]{1,0:T(8,128)(2,1)S(1)} custom-call(s32[16]{0:T(128)S(1)} %bitcast.15, f32[16,64,64]{2,1,0:T(8,128)} %bitcast.16, bf16[16,32,128]{2,1,0:T(8,128)(2,1)} %up.1.after_ref), custom_call_target="tpu_custom_call" | custom-call | flops 100000000 | bytes 1048576 | tf_op jit(solution)/shard_map/weights/pallas_call | solution.py:206
  20.8 0.0 copy-done
  20.8 2.9 %collective-permute-start.1 = (bf16[2,128,256]{2,1,0:T(8,128)(2,1)S(1)}, bf16[2,128,256]{2,1,0:T(8,128)(2,1)S(1)}, u32[]{:S(2)}, u32[]{:S(2)}) collective-permute-start(bf16[2,128,256]{2,1,0:T(8,128)(2,1)S(1)} %get-tuple-element.11), channel_id=1, source_target_pairs={{16,0},{32,16},{48,32},{64,48},{80,64},{96,80},{112,96},{128,112},... | collective-permute-start | bytes 393224 | tf_op jit(solution)/shard_map/ppermute | solution.py:308
  23.7 3.1 %collective-permute-start = (bf16[2,128,256]{2,1,0:T(8,128)(2,1)S(1)}, bf16[2,128,256]{2,1,0:T(8,128)(2,1)S(1)}, u32[]{:S(2)}, u32[]{:S(2)}) collective-permute-start(bf16[2,128,256]{2,1,0:T(8,128)(2,1)S(1)} %get-tuple-element.12), channel_id=1, source_target_pairs={{0,16},{16,32},{32,48},{48,64},{64,80},{80,96},{96,112},{112,128},... | collective-permute-start | bytes 393224 | tf_op jit(solution)/shard_map/ppermute | solution.py:307
  26.8 1.0 %collective-permute-done.1.after_ref = bf16[2,128,256]{2,1,0:T(8,128)(2,1)S(1)} collective-permute-done((bf16[2,128,256]{2,1,0:T(8,128)(2,1)S(1)}, bf16[2,128,256]{2,1,0:T(8,128)(2,1)S(1)}, u32[]{:S(2)}, u32[]{:S(2)}) %collective-permute-start.1) | collective-permute-done | bytes 131104 | tf_op jit(solution)/shard_map/ppermute | solution.py:308
  27.8 0.9 %collective-permute-done.before_ref = bf16[2,128,256]{2,1,0:T(8,128)(2,1)S(1)} collective-permute-done((bf16[2,128,256]{2,1,0:T(8,128)(2,1)S(1)}, bf16[2,128,256]{2,1,0:T(8,128)(2,1)S(1)}, u32[]{:S(2)}, u32[]{:S(2)}) %collective-permute-start) | collective-permute-done | bytes 131104 | tf_op jit(solution)/shard_map/ppermute | solution.py:307
  28.7 1.8 %all-to-all-done.in_ref = bf16[16,32,128]{2,1,0:T(8,128)(2,1)S(1)} async-done(((bf16[16,32,128]{2,1,0:T(8,128)(2,1)}), bf16[16,32,128]{2,1,0:T(8,128)(2,1)S(1)}, u32[]{:S(2)}, u32[]{:S(2)}) %all-to-all-start) | async-done | bytes 131104 | tf_op jit(solution)/shard_map/all_to_all | solution.py:306
  30.5 0.7 %sum.1.after_sum_ref = bf16[32,32,128]{2,1,0:T(8,128)(2,1)} custom-call(bf16[16,32,128]{2,1,0:T(8,128)(2,1)S(1)} %all-to-all-done.in_ref, bf16[2,128,256]{2,1,0:T(8,128)(2,1)S(1)} %collective-permute-done.before_ref, bf16[2,128,256]{2,1,0:T(8,128)(2,1)S(1)} %collective-permute-done.1.after_ref), custom_call_target="tpu_custom_call" | custom-call | flops 10000000 | bytes 524288 | tf_op jit(solution)/shard_map/sum/pallas_call | solution.py:206
  31.3 10.7 %all-to-all-start.1 = ((bf16[32,32,128]{2,1,0:T(8,128)(2,1)}), bf16[32,32,128]{2,1,0:T(8,128)(2,1)S(1)}, u32[]{:S(2)}, u32[]{:S(2)}) async-start(bf16[32,32,128]{2,1,0:T(8,128)(2,1)} %sum.1.after_sum_ref), calls=%async_computation.1 | async-start | bytes 524288 | tf_op jit(solution)/shard_map/all_to_all | solution.py:322
  42.0 0.1 rim.1
  42.1 3.1 %collective-permute-start.2 = (bf16[6,128,256]{2,1,0:T(8,128)(2,1)S(1)}, bf16[6,128,256]{2,1,0:T(8,128)(2,1)S(1)}, u32[]{:S(2)}, u32[]{:S(2)}) collective-permute-start(bf16[6,128,256]{2,1,0:T(8,128)(2,1)S(1)} %get-tuple-element.9), channel_id=1, source_target_pairs={{0,1},{1,2},{2,3},{3,4},{4,5},{5,6},{6,7},{7,8},{8,9},{9,10},{10,1... | collective-permute-start | bytes 1179656 | tf_op jit(solution)/shard_map/ppermute | solution.py:323
  45.2 0.0 copy-start.2
  45.2 1.3 %collective-permute-start.3 = (bf16[6,128,256]{2,1,0:T(8,128)(2,1)S(1)}, bf16[6,128,256]{2,1,0:T(8,128)(2,1)S(1)}, u32[]{:S(2)}, u32[]{:S(2)}) collective-permute-start(bf16[6,128,256]{2,1,0:T(8,128)(2,1)S(1)} %get-tuple-element.10), channel_id=1, source_target_pairs={{1,0},{2,1},{3,2},{4,3},{5,4},{6,5},{7,6},{8,7},{9,8},{10,9},{11,1... | collective-permute-start | bytes 1179656 | tf_op jit(solution)/shard_map/ppermute | solution.py:324
  46.5 4.5 %all-to-all-done.1.tops_ref = bf16[32,32,128]{2,1,0:T(8,128)(2,1)S(1)} async-done(((bf16[32,32,128]{2,1,0:T(8,128)(2,1)}), bf16[32,32,128]{2,1,0:T(8,128)(2,1)S(1)}, u32[]{:S(2)}, u32[]{:S(2)}) %all-to-all-start.1) | async-done | bytes 262176 | tf_op jit(solution)/shard_map/all_to_all | solution.py:322
  51.0 1.0 %couple.1 = bf16[4,32,128]{2,1,0:T(8,128)(2,1)} custom-call(bf16[32,32,128]{2,1,0:T(8,128)(2,1)S(1)} %all-to-all-done.1.tops_ref, bf16[256,1024]{1,0:T(8,128)(2,1)S(1)} %weights.1.weights_ref), custom_call_target="tpu_custom_call" | custom-call | flops 30000001024 | bytes 524288 | tf_op jit(solution)/shard_map/couple/pallas_call | solution.py:206
  52.0 3.3 %all-to-all-start.2 = ((bf16[4,32,128]{2,1,0:T(8,128)(2,1)}), bf16[4,32,128]{2,1,0:T(8,128)(2,1)S(1)}, u32[]{:S(2)}, u32[]{:S(2)}) async-start(bf16[4,32,128]{2,1,0:T(8,128)(2,1)} %couple.1), calls=%async_computation.2 | async-start | bytes 65536 | tf_op jit(solution)/shard_map/all_to_all | solution.py:336
  55.3 0.0 copy-done.2
  55.3 0.1 reshape.21.lists_ref
  55.3 1.4 %hold.1.blocks_ref = bf16[4,2,6,128,128]{4,3,2,1,0:T(8,128)(2,1)S(1)} custom-call(bf16[4,2,6,128,128]{4,3,2,1,0:T(8,128)(2,1)} %blocks_ref.1, bf16[16,32,128]{2,1,0:T(8,128)(2,1)} %up.1.after_ref), custom_call_target="tpu_custom_call" | custom-call | flops 1000000 | bytes 2097152 | tf_op jit(solution)/shard_map/hold/pallas_call | solution.py:206
  56.8 2.4 %far.1.far_ref = bf16[1024,128]{1,0:T(8,128)(2,1)S(1)} custom-call(f32[4,2,64,64]{3,2,1,0:T(8,128)} %bitcast.19, f32[8,64,64]{2,1,0:T(8,128)} %bitcast.20, bf16[8,64,128]{2,1,0:T(8,128)(2,1)} %bitcast.22, bf16[16,32,128]{2,1,0:T(8,128)(2,1)} %up.1.after_ref), custom_call_target="tpu_custom_call" | custom-call | flops 100000000 | bytes 1048576 | tf_op jit(solution)/shard_map/far/pallas_call | solution.py:206
  59.2 0.0 collective-permute-done.2.left_ref
  59.2 0.0 collective-permute-done.3.right_ref
  59.2 1.2 %near.1.near_ref = f32[8,128,256]{2,1,0:T(8,128)S(1)} custom-call(s32[48]{0:T(128)S(1)} %reshape.21.lists_ref, bf16[4,2,128,256]{3,2,1,0:T(8,128)(2,1)S(1)} %copy-done, bf16[2,128,256]{2,1,0:T(8,128)(2,1)S(1)} %collective-permute-done.before_ref, bf16[2,128,256]{2,1,0:T(8,128)(2,1)S(1)} %collective-permute-done.1.after_ref, ...), custom_call_target="tpu_custom_call" | custom-call | flops 402653184 | bytes 4194304 | tf_op jit(solution)/shard_map/near/pallas_call | solution.py:206
  60.4 0.0 all-to-all-done.2.coeff_ref
  60.4 1.1 %final.1 = bf16[8,128,256]{2,1,0:T(8,128)(2,1)} custom-call(f32[8,128,256]{2,1,0:T(8,128)S(1)} %near.1.near_ref, bf16[1024,128]{1,0:T(8,128)(2,1)S(1)} %far.1.far_ref, bf16[4,32,128]{2,1,0:T(8,128)(2,1)S(1)} %all-to-all-done.2.coeff_ref), custom_call_target="tpu_custom_call" | custom-call | flops 67108864 | bytes 2097152 | tf_op jit(solution)/shard_map/final/pallas_call | solution.py:206
  (1 shorter events, 0.0 us)
Async XLA Ops:
  0.0 20.8 %copy-start = (bf16[4,2,128,256]{3,2,1,0:T(8,128)(2,1)S(1)}, bf16[4,2,128,256]{3,2,1,0:T(8,128)(2,1)}, u32[]{:S(2)}) copy-start(bf16[4,2,128,256]{3,2,1,0:T(8,128)(2,1)} %slip_ref.1) | copy-start | bytes 1572868
  0.0 18.5 %copy-start.1 = (s32[1,16]{1,0:T(1,128)S(1)}, s32[1,16]{1,0:T(1,128)}, u32[]{:S(2)}) copy-start(s32[1,16]{1,0:T(1,128)} %param.20) | copy-start | bytes 196
  2.8 27.8 %all-to-all-start = ((bf16[16,32,128]{2,1,0:T(8,128)(2,1)}), bf16[16,32,128]{2,1,0:T(8,128)(2,1)S(1)}, u32[]{:S(2)}, u32[]{:S(2)}) async-start(bf16[16,32,128]{2,1,0:T(8,128)(2,1)} %up.1.after_ref), calls=%async_computation | async-start | bytes 262144 | tf_op jit(solution)/shard_map/all_to_all | solution.py:306
  20.8 7.0 %collective-permute-start.1 = (bf16[2,128,256]{2,1,0:T(8,128)(2,1)S(1)}, bf16[2,128,256]{2,1,0:T(8,128)(2,1)S(1)}, u32[]{:S(2)}, u32[]{:S(2)}) collective-permute-start(bf16[2,128,256]{2,1,0:T(8,128)(2,1)S(1)} %get-tuple-element.11), channel_id=1, source_target_pairs={{16,0},{32,16},{48,32},{64,48},{80,64},{96,80},{112,96},{128,112},... | collective-permute-start | bytes 393224 | tf_op jit(solution)/shard_map/ppermute | solution.py:308
  23.7 5.0 %collective-permute-start = (bf16[2,128,256]{2,1,0:T(8,128)(2,1)S(1)}, bf16[2,128,256]{2,1,0:T(8,128)(2,1)S(1)}, u32[]{:S(2)}, u32[]{:S(2)}) collective-permute-start(bf16[2,128,256]{2,1,0:T(8,128)(2,1)S(1)} %get-tuple-element.12), channel_id=1, source_target_pairs={{0,16},{16,32},{32,48},{48,64},{64,80},{80,96},{96,112},{112,128},... | collective-permute-start | bytes 393224 | tf_op jit(solution)/shard_map/ppermute | solution.py:307
  31.3 19.7 %all-to-all-start.1 = ((bf16[32,32,128]{2,1,0:T(8,128)(2,1)}), bf16[32,32,128]{2,1,0:T(8,128)(2,1)S(1)}, u32[]{:S(2)}, u32[]{:S(2)}) async-start(bf16[32,32,128]{2,1,0:T(8,128)(2,1)} %sum.1.after_sum_ref), calls=%async_computation.1 | async-start | bytes 524288 | tf_op jit(solution)/shard_map/all_to_all | solution.py:322
  42.1 17.1 %collective-permute-start.2 = (bf16[6,128,256]{2,1,0:T(8,128)(2,1)S(1)}, bf16[6,128,256]{2,1,0:T(8,128)(2,1)S(1)}, u32[]{:S(2)}, u32[]{:S(2)}) collective-permute-start(bf16[6,128,256]{2,1,0:T(8,128)(2,1)S(1)} %get-tuple-element.9), channel_id=1, source_target_pairs={{0,1},{1,2},{2,3},{3,4},{4,5},{5,6},{6,7},{7,8},{8,9},{9,10},{10,1... | collective-permute-start | bytes 1179656 | tf_op jit(solution)/shard_map/ppermute | solution.py:323
  45.2 10.1 %copy-start.2 = (s32[4,2,6]{2,1,0:T(2,128)S(1)}, s32[4,2,6]{2,1,0:T(2,128)}, u32[]{:S(2)}) copy-start(s32[4,2,6]{2,1,0:T(2,128)} %param.12) | copy-start | bytes 580
  45.2 14.0 %collective-permute-start.3 = (bf16[6,128,256]{2,1,0:T(8,128)(2,1)S(1)}, bf16[6,128,256]{2,1,0:T(8,128)(2,1)S(1)}, u32[]{:S(2)}, u32[]{:S(2)}) collective-permute-start(bf16[6,128,256]{2,1,0:T(8,128)(2,1)S(1)} %get-tuple-element.10), channel_id=1, source_target_pairs={{1,0},{2,1},{3,2},{4,3},{5,4},{6,5},{7,6},{8,7},{9,8},{10,9},{11,1... | collective-permute-start | bytes 1179656 | tf_op jit(solution)/shard_map/ppermute | solution.py:324
  52.0 8.4 %all-to-all-start.2 = ((bf16[4,32,128]{2,1,0:T(8,128)(2,1)}), bf16[4,32,128]{2,1,0:T(8,128)(2,1)S(1)}, u32[]{:S(2)}, u32[]{:S(2)}) async-start(bf16[4,32,128]{2,1,0:T(8,128)(2,1)} %couple.1), calls=%async_computation.2 | async-start | bytes 65536 | tf_op jit(solution)/shard_map/all_to_all | solution.py:336

commit v2 on v1

--- a/solution.py
+++ b/solution.py
@@ -8,6 +8,8 @@
 F32 = jnp.float32
 BF16 = jnp.bfloat16
 QUARTERS = 4
+COL_FIRST = 11
+ROW_FIRST = 31
 
 
 def halves(value):
@@ -63,50 +65,47 @@
     s0, s1, s2, s3 = chain_of(strip_up, lax.axis_index("col"), 4)
     chain = dot_split(dot_split(s3, s2), dot_split(s1, s0))
     copies[1].wait()
-    ups = jnp.concatenate([leaf_up[leaf] for leaf in range(leaves)], axis=1)
+    ups = dot_split(chain, jnp.concatenate([leaf_up[leaf] for leaf in range(leaves)], axis=1))
     copies[2].wait()
     copies[3].wait()
     moments = jnp.concatenate([dot(basis[leaf], slip[leaf]) for leaf in range(leaves)], axis=0)
-    node = dot_split(chain, dot_split(ups, moments))
+    node = dot_split(ups, moments)
     for quarter in range(QUARTERS):
         half = quarter // 2
         packed = pack(node[:, 128 * half : 128 * (half + 1)], quarter % 2).astype(BF16)
         for copy in range(out_ref.shape[0] // QUARTERS):
-            out_ref[copy * QUARTERS + quarter] = packed
-
-
-def sum_kernel(in_ref, before_ref, after_ref, out_ref):
-    del before_ref, after_ref
+            out_ref[copy * QUARTERS + (quarter - COL_FIRST) % QUARTERS] = packed
+
+
+def sum_kernel(in_ref, after_ref, out_ref):
+    del after_ref
     total = jnp.sum(in_ref[...].astype(F32), axis=0).astype(BF16)
     for copy in range(out_ref.shape[0]):
         out_ref[copy] = total
 
 
-def weights_kernel(lists_ref, coupling_ref, after_ref, out_ref, coupling, wide, sems):
+def weights_kernel(lists_ref, coupling_ref, after_ref, out_ref, wide):
     del after_ref
-    (copy,) = fetch((coupling_ref,), (coupling,), sems)
-    strips, rank = coupling.shape[0], coupling.shape[1]
+    strips, rank = coupling_ref.shape[0], coupling_ref.shape[1]
     half = rank // 2
     columns = out_ref.shape[1]
     row = lax.broadcasted_iota(jnp.int32, (half, columns), 0)
     column = lax.broadcasted_iota(jnp.int32, (half, columns), 1)
-    chosen = [
-        jnp.where(column == row + lists_ref[strip] * half, 1.0, 0.0).astype(BF16) for strip in range(strips)
-    ]
-    copy.wait()
+    chosen = []
+    for strip in range(strips):
+        place = (ROW_FIRST - lists_ref[strip]) & (columns // half - 1)
+        chosen.append(jnp.where(column == row + place * half, 1.0, 0.0).astype(BF16))
     for strip in range(strips):
         at = slice(strip * half, (strip + 1) * half)
-        wide[0:rank, at] = coupling[strip, :, 0:half]
-        wide[rank : 2 * rank, at] = coupling[strip, :, half:rank]
+        wide[0:rank, at] = coupling_ref[strip, :, 0:half]
+        wide[rank : 2 * rank, at] = coupling_ref[strip, :, half:rank]
     high, low = halves(wide[...])
     both = dot(jnp.concatenate([high, low], axis=0), jnp.concatenate(chosen, axis=0))
     out_ref[...] = both.astype(BF16)
 
 
-def far_kernel(strip_down_ref, leaf_down_ref, target_ref, after_ref, out_ref, strip_down, leaf_down, target, sems):
+def far_kernel(strip_down, leaf_down, target, after_ref, out_ref):
     del after_ref
-    for copy in fetch((strip_down_ref, leaf_down_ref, target_ref), (strip_down, leaf_down, target), sems):
-        copy.wait()
     s0, s1, s2, s3 = chain_of(strip_down, lax.axis_index("col"), 4)
     chain = dot_split(dot_split(s0, s1), dot_split(s2, s3))
     leaves, rank, size = target.shape
@@ -140,6 +139,12 @@
     ).astype(BF16)
     for copy in range(out_ref.shape[0]):
         out_ref[copy] = packed
+
+
+def edges_kernel(slip_ref, after_ref, first_ref, last_ref):
+    del after_ref
+    first_ref[...] = slip_ref[0]
+    last_ref[...] = slip_ref[slip_ref.shape[0] - 1]
 
 
 def rim_kernel(slip_ref, before_ref, after_ref, after_sum_ref, left_ref, right_ref):
@@ -182,8 +187,8 @@
     left = lax.broadcasted_iota(jnp.int32, (rows, lanes), 1) < lanes // 2
     tiles = []
     for half in range(2):
-        one = coeff_ref[2 * half].astype(F32)
-        two = coeff_ref[2 * half + 1].astype(F32)
+        one = coeff_ref[QUARTERS - 1 - 2 * half].astype(F32)
+        two = coeff_ref[QUARTERS - 2 - 2 * half].astype(F32)
         upper = jnp.where(left, one, pltpu.roll(two, lanes // 2, 1))
         lower = jnp.where(left, pltpu.roll(one, lanes // 2, 1), two)
         tiles.append(jnp.concatenate([upper, lower], axis=0).astype(BF16))
@@ -261,57 +266,32 @@
         flops=100_000_000,
         size=2 * mega,
     )
-    weights = call(
-        weights_kernel,
-        sds((4 * rank, n_row * rank // 2), BF16),
-        "sha",
-        strip_lists[0],
-        couplings,
-        parts,
-        scratch=[room(couplings), pltpu.VMEM((2 * rank, strips * rank // 2), F32), dma((1,))],
-        name="weights",
-        flops=100_000_000,
-        size=mega,
-    )
-    far = call(
-        far_kernel,
-        sds((leaves * size, 2 * rank), BF16),
-        "hhha",
-        strip_down[0],
-        downs,
-        target,
-        parts,
-        scratch=[room(strip_down[0]), room(downs), room(target), dma((3,))],
-        name="far",
-        flops=100_000_000,
-        size=mega,
-    )
-    blocks = call(
-        hold_kernel,
-        sds(near_blocks.shape, BF16),
-        "ha",
-        near_blocks,
-        parts,
-        scratch=[dma((1,))],
-        name="hold",
-        flops=1_000_000,
-        size=2 * mega,
-    )
-    held, _ = lax.optimization_barrier((slip_rate, weights))
     up_row = [(i, i + 1) for i in range(n_row - 1)]
     down_row = [(j, i) for i, j in up_row]
     up_col = [(i, i + 1) for i in range(n_col - 1)]
     down_col = [(j, i) for i, j in up_col]
 
-    parts = lax.all_to_all(parts, "col", 0, 0, tiled=True)
-    before = lax.ppermute(held[along - 1], "row", up_row)
-    after = lax.ppermute(held[0], "row", down_row)
-    tops = call(sum_kernel, sds((n_row, *piece), BF16), "vaa", parts, before, after, name="sum", flops=10_000_000, size=mega // 2)
+    edge = sds((dip, size, members), BF16)
+    first, last = call(
+        edges_kernel,
+        (edge, edge),
+        "va",
+        slip_rate,
+        parts,
+        name="edges",
+        flops=10_000_000_000,
+        size=mega,
+    )
+    before = lax.ppermute(last, "row", up_row)
+    after = lax.ppermute(first, "row", down_row)
+    turned = [(i + COL_FIRST) % n_col for i in range(n_col)]
+    parts = lax.all_to_all(parts, "col", 0, 0, tiled=True, axis_index_groups=[turned])
+    tops = call(sum_kernel, sds((n_row, *piece), BF16), "va", parts, first, name="sum", flops=30_000_000_000, size=mega // 2)
     rim_left, rim_right = call(
         rim_kernel,
         (sds((along + 2, size, members), BF16), sds((along + 2, size, members), BF16)),
         "vvva",
-        held,
+        slip_rate,
         before,
         after,
         tops,
@@ -319,7 +299,20 @@
         flops=1_000_000,
         size=mega,
     )
-    tops = lax.all_to_all(tops, "row", 0, 0, tiled=True)
+    weights = call(
+        weights_kernel,
+        sds((4 * rank, n_row * rank // 2), BF16),
+        "sva",
+        strip_lists[0],
+        couplings,
+        rim_left,
+        scratch=[pltpu.VMEM((2 * rank, strips * rank // 2), F32)],
+        name="weights",
+        flops=30_000_000_000,
+        size=mega,
+    )
+    order = [(ROW_FIRST - i) % n_row for i in range(n_row)]
+    tops = lax.all_to_all(tops, "row", 0, 0, tiled=True, axis_index_groups=[order])
     from_left = lax.ppermute(rim_right, "col", up_col)
     from_right = lax.ppermute(rim_left, "col", down_col)
     coeff = call(
@@ -332,14 +325,37 @@
         flops=30_000_000_000,
         size=mega // 2,
     )
-    groups = [list(range(i, i + QUARTERS)) for i in range(0, n_col, QUARTERS)]
+    far = call(
+        far_kernel,
+        sds((leaves * size, 2 * rank), BF16),
+        "vvva",
+        strip_down[0],
+        downs,
+        target,
+        coeff,
+        name="far",
+        flops=100_000_000,
+        size=mega,
+    )
+    blocks = call(
+        hold_kernel,
+        sds(near_blocks.shape, BF16),
+        "ha",
+        near_blocks,
+        coeff,
+        scratch=[dma((1,))],
+        name="hold",
+        flops=1_000_000,
+        size=2 * mega,
+    )
+    groups = [list(range(i, i + QUARTERS))[::-1] for i in range(0, n_col, QUARTERS)]
     coeff = lax.all_to_all(coeff, "col", 0, 0, tiled=True, axis_index_groups=groups)
     near = call(
         near_kernel,
         sds((leaves, size, members), F32),
         "svvvvvv",
         near_lists.reshape(-1),
-        held,
+        slip_rate,
         before,
         after,
         from_left,

time: 62.1 us -> 57.5 us (0.926)
  waiting for transfers between devices: 8.25 us -> 2.27 us
  starting transfers between devices: 40.1 us -> 42.8 us
  Pallas kernels: 12.9 us -> 11.7 us
    all_to_all x2, waiting for transfers between devices: 6.31 us -> 2.26 us  [the longest x1 2.26 us: body(): lax.all_to_all(parts, 'col', 0, 0, tiled=True, axis_index_groups=[turned])]
    ppermute x2, waiting for transfers between devices: 1.93 us -> 0.01 us  [the longest x1 0.01 us: body(): after = lax.ppermute(first, 'row', down_row)]
    all_to_all x1, starting transfers between devices: 3.26 us -> 4.8 us  [body(): lax.all_to_all(coeff, 'col', 0, 0, tiled=True, axis_index_groups=groups)]
    pallas_call x9 -> x10, Pallas kernels: 12.9 us -> 11.7 us  [call(): pl.pallas_call(kernel, out_shape=outs, in_specs=[pl.BlockSpec(memory_spac...]
    ppermute x1, starting transfers between devices: 3.1 us -> 4.01 us  [body(): from_left = lax.ppermute(rim_right, 'col', up_col)]
  transfers between devices with their start and end apart: 7 -> 7, of which waited for: 4 -> 1; matrix products, arithmetic and copies ran while one was open for 0% -> 0% of each run, Pallas kernels for 13% -> 14%
where the time goes in v2:
time: 57.5 us; the launch traced here: 57.1 us
  starting transfers between devices  42.8 us (74%)
  Pallas kernels  11.7 us (20%)
  waiting for transfers between devices  2.27 us (4%)
    all_to_all x1, starting transfers between devices, body(): lax.all_to_all(parts, 'col', 0, 0, tiled=True, axis_index_groups=[turned])  16.4 us
    pallas_call x10, Pallas kernels, call(): pl.pallas_call(kernel, out_shape=outs, in_specs=[pl.BlockSpec(memory_spac...  11.7 us
    all_to_all x1, starting transfers between devices, body(): lax.all_to_all(tops, 'row', 0, 0, tiled=True, axis_index_groups=[order])  10.1 us
    all_to_all x1, starting transfers between devices, body(): lax.all_to_all(coeff, 'col', 0, 0, tiled=True, axis_index_groups=groups)  4.8 us
    ppermute x1, starting transfers between devices, body(): from_left = lax.ppermute(rim_right, 'col', up_col)  4.01 us
    ppermute x1, starting transfers between devices, body(): after = lax.ppermute(first, 'row', down_row)  3.14 us
    ppermute x1, starting transfers between devices, body(): before = lax.ppermute(last, 'row', up_row)  3.1 us
    all_to_all x1, waiting for transfers between devices, body(): lax.all_to_all(parts, 'col', 0, 0, tiled=True, axis_index_groups=[turned])  2.26 us
  transfers between devices with their start and end apart: 7, of which 1 were waited for; matrix products, arithmetic and copies ran while one was open for 0% of the time, Pallas kernels for 14%

profile of v2, /device:TPU:1, one launch (start us, length us, event | category | flops | bytes accessed | tf_op | source)
XLA Modules:
  0.0 57.1 jit_solution(8575851193236931800)
XLA Ops:
  0.0 0.0 copy-start
  0.0 2.8 %up.1.after_ref = bf16[16,32,128]{2,1,0:T(8,128)(2,1)} custom-call(f32[4,2,64,64]{3,2,1,0:T(8,128)} %bitcast.16, f32[8,64,64]{2,1,0:T(8,128)} %bitcast.17, bf16[8,64,128]{2,1,0:T(8,128)(2,1)} %bitcast.18, bf16[8,128,256]{2,1,0:T(8,128)(2,1)} %bitcast.10), custom_call_target="tpu_custom_call" | custom-call | flops 100000000 | bytes 2097152 | tf_op jit(solution)/shard_map/up/pallas_call | solution.py:211
  2.8 16.4 %all-to-all-start = ((bf16[16,32,128]{2,1,0:T(8,128)(2,1)}), bf16[16,32,128]{2,1,0:T(8,128)(2,1)S(1)}, u32[]{:S(2)}, u32[]{:S(2)}) async-start(bf16[16,32,128]{2,1,0:T(8,128)(2,1)} %up.1.after_ref), calls=%async_computation | async-start | bytes 262144 | tf_op jit(solution)/shard_map/all_to_all | solution.py:288
  19.2 0.0 copy-done
  19.3 3.1 %collective-permute-start.1 = (bf16[2,128,256]{2,1,0:T(8,128)(2,1)S(1)}, bf16[2,128,256]{2,1,0:T(8,128)(2,1)S(1)}, u32[]{:S(2)}, u32[]{:S(2)}) collective-permute-start(bf16[2,128,256]{2,1,0:T(8,128)(2,1)S(1)} %get-tuple-element.10.after_ref), channel_id=1, source_target_pairs={{16,0},{32,16},{48,32},{64,48},{80,64},{96,80},{112,96},{128,112},... | collective-permute-start | bytes 393224 | tf_op jit(solution)/shard_map/ppermute | solution.py:286
  22.4 3.1 %collective-permute-start = (bf16[2,128,256]{2,1,0:T(8,128)(2,1)S(1)}, bf16[2,128,256]{2,1,0:T(8,128)(2,1)S(1)}, u32[]{:S(2)}, u32[]{:S(2)}) collective-permute-start(bf16[2,128,256]{2,1,0:T(8,128)(2,1)S(1)} %get-tuple-element.9), channel_id=1, source_target_pairs={{0,16},{16,32},{32,48},{48,64},{64,80},{80,96},{96,112},{112,128},... | collective-permute-start | bytes 393224 | tf_op jit(solution)/shard_map/ppermute | solution.py:285
  25.5 2.3 %all-to-all-done.in_ref = bf16[16,32,128]{2,1,0:T(8,128)(2,1)S(1)} async-done(((bf16[16,32,128]{2,1,0:T(8,128)(2,1)}), bf16[16,32,128]{2,1,0:T(8,128)(2,1)S(1)}, u32[]{:S(2)}, u32[]{:S(2)}) %all-to-all-start) | async-done | bytes 131104 | tf_op jit(solution)/shard_map/all_to_all | solution.py:288
  27.8 0.7 %sum.1.after_sum_ref = bf16[32,32,128]{2,1,0:T(8,128)(2,1)} custom-call(bf16[16,32,128]{2,1,0:T(8,128)(2,1)S(1)} %all-to-all-done.in_ref, bf16[2,128,256]{2,1,0:T(8,128)(2,1)S(1)} %get-tuple-element.10.after_ref), custom_call_target="tpu_custom_call" | custom-call | flops 30000001024 | bytes 524288 | tf_op jit(solution)/shard_map/sum/pallas_call | solution.py:211
  28.5 0.0 copy-start.4
  28.5 0.0 copy-start.5
  28.5 10.1 %all-to-all-start.1 = ((bf16[32,32,128]{2,1,0:T(8,128)(2,1)}), bf16[32,32,128]{2,1,0:T(8,128)(2,1)S(1)}, u32[]{:S(2)}, u32[]{:S(2)}) async-start(bf16[32,32,128]{2,1,0:T(8,128)(2,1)} %sum.1.after_sum_ref), calls=%async_computation.1 | async-start | bytes 524288 | tf_op jit(solution)/shard_map/all_to_all | solution.py:315
  38.6 0.0 collective-permute-done.1.after_ref
  38.6 0.0 collective-permute-done.before_ref
  38.6 0.8 %rim.1 = (bf16[6,128,256]{2,1,0:T(8,128)(2,1)}, bf16[6,128,256]{2,1,0:T(8,128)(2,1)S(1)}) custom-call(bf16[4,2,128,256]{3,2,1,0:T(8,128)(2,1)S(1)} %copy-done, bf16[2,128,256]{2,1,0:T(8,128)(2,1)S(1)} %collective-permute-done.before_ref, bf16[2,128,256]{2,1,0:T(8,128)(2,1)S(1)} %collective-permute-done.1.after_ref, bf16[32,32,128]{2,1,0:T(8,128)(2,1)} %sum.1.after_sum_ref), custom_call_target="tpu_custom_call" | custom-call | flops 1000000 | bytes 1048576 | tf_op jit(solution)/shard_map/rim/pallas_call | solution.py:211
  39.4 1.3 %collective-permute-start.3 = (bf16[6,128,256]{2,1,0:T(8,128)(2,1)}, bf16[6,128,256]{2,1,0:T(8,128)(2,1)S(1)}, u32[]{:S(2)}, u32[]{:S(2)}) collective-permute-start(bf16[6,128,256]{2,1,0:T(8,128)(2,1)} %get-tuple-element.12.after_ref), channel_id=1, source_target_pairs={{1,0},{2,1},{3,2},{4,3},{5,4},{6,5},{7,6},{8,7},{9,8},{10,9},{11,1... | collective-permute-start | bytes 1179656 | tf_op jit(solution)/shard_map/ppermute | solution.py:317
  40.7 4.0 %collective-permute-start.2 = (bf16[6,128,256]{2,1,0:T(8,128)(2,1)S(1)}, bf16[6,128,256]{2,1,0:T(8,128)(2,1)S(1)}, u32[]{:S(2)}, u32[]{:S(2)}) collective-permute-start(bf16[6,128,256]{2,1,0:T(8,128)(2,1)S(1)} %get-tuple-element.11), channel_id=1, source_target_pairs={{0,1},{1,2},{2,3},{3,4},{4,5},{5,6},{6,7},{7,8},{8,9},{9,10},{10,1... | collective-permute-start | bytes 1179656 | tf_op jit(solution)/shard_map/ppermute | solution.py:316
  44.7 0.0 copy-done.4
  44.7 0.0 copy-done.5
  44.7 1.2 %weights.1.weights_ref = bf16[256,1024]{1,0:T(8,128)(2,1)S(1)} custom-call(s32[16]{0:T(128)S(1)} %bitcast.15, f32[16,64,64]{2,1,0:T(8,128)S(1)} %bitcast.14, bf16[6,128,256]{2,1,0:T(8,128)(2,1)} %get-tuple-element.12.after_ref), custom_call_target="tpu_custom_call" | custom-call | flops 30000001024 | bytes 1048576 | tf_op jit(solution)/shard_map/weights/pallas_call | solution.py:211
  45.9 0.0 copy-start.6
  46.0 0.0 all-to-all-done.1.tops_ref
  46.0 1.0 %couple.1.after_ref = bf16[4,32,128]{2,1,0:T(8,128)(2,1)} custom-call(bf16[32,32,128]{2,1,0:T(8,128)(2,1)S(1)} %all-to-all-done.1.tops_ref, bf16[256,1024]{1,0:T(8,128)(2,1)S(1)} %weights.1.weights_ref), custom_call_target="tpu_custom_call" | custom-call | flops 30000001024 | bytes 524288 | tf_op jit(solution)/shard_map/couple/pallas_call | solution.py:211
  46.9 4.8 %all-to-all-start.2 = ((bf16[4,32,128]{2,1,0:T(8,128)(2,1)}), bf16[4,32,128]{2,1,0:T(8,128)(2,1)S(1)}, u32[]{:S(2)}, u32[]{:S(2)}) async-start(bf16[4,32,128]{2,1,0:T(8,128)(2,1)} %couple.1.after_ref), calls=%async_computation.2 | async-start | bytes 65536 | tf_op jit(solution)/shard_map/all_to_all | solution.py:352
  51.7 0.0 copy-done.6
  51.7 0.1 reshape.21.lists_ref
  51.8 0.0 copy-start.1
  51.8 0.0 copy-start.2
  51.8 0.0 copy-start.3
  51.8 1.5 %hold.1.blocks_ref = bf16[4,2,6,128,128]{4,3,2,1,0:T(8,128)(2,1)S(1)} custom-call(bf16[4,2,6,128,128]{4,3,2,1,0:T(8,128)(2,1)} %blocks_ref.1, bf16[4,32,128]{2,1,0:T(8,128)(2,1)} %couple.1.after_ref), custom_call_target="tpu_custom_call" | custom-call | flops 1000000 | bytes 2097152 | tf_op jit(solution)/shard_map/hold/pallas_call | solution.py:211
  53.3 0.0 copy-done.1
  53.3 0.0 copy-done.2
  53.3 0.0 copy-done.3
  53.4 1.3 %far.1.far_ref = bf16[1024,128]{1,0:T(8,128)(2,1)S(1)} custom-call(f32[4,2,64,64]{3,2,1,0:T(8,128)S(1)} %bitcast.11, f32[8,64,64]{2,1,0:T(8,128)S(1)} %bitcast.12, bf16[8,64,128]{2,1,0:T(8,128)(2,1)S(1)} %bitcast.13, bf16[4,32,128]{2,1,0:T(8,128)(2,1)} %couple.1.after_ref), custom_call_target="tpu_custom_call" | custom-call | flops 100000000 | bytes 1048576 | tf_op jit(solution)/shard_map/far/pallas_call | solution.py:211
  54.7 0.0 collective-permute-done.3.right_ref
  54.7 0.0 collective-permute-done.2.left_ref
  54.7 1.3 %near.1.near_ref = f32[8,128,256]{2,1,0:T(8,128)S(1)} custom-call(s32[48]{0:T(128)S(1)} %reshape.21.lists_ref, bf16[4,2,128,256]{3,2,1,0:T(8,128)(2,1)S(1)} %copy-done, bf16[2,128,256]{2,1,0:T(8,128)(2,1)S(1)} %collective-permute-done.before_ref, bf16[2,128,256]{2,1,0:T(8,128)(2,1)S(1)} %collective-permute-done.1.after_ref, ...), custom_call_target="tpu_custom_call" | custom-call | flops 402653184 | bytes 4194304 | tf_op jit(solution)/shard_map/near/pallas_call | solution.py:211
  56.0 0.0 all-to-all-done.2.coeff_ref
  56.0 1.1 %final.1 = bf16[8,128,256]{2,1,0:T(8,128)(2,1)} custom-call(f32[8,128,256]{2,1,0:T(8,128)S(1)} %near.1.near_ref, bf16[1024,128]{1,0:T(8,128)(2,1)S(1)} %far.1.far_ref, bf16[4,32,128]{2,1,0:T(8,128)(2,1)S(1)} %all-to-all-done.2.coeff_ref), custom_call_target="tpu_custom_call" | custom-call | flops 67108864 | bytes 2097152 | tf_op jit(solution)/shard_map/final/pallas_call | solution.py:211
  (1 shorter events, 0.0 us)
Async XLA Ops:
  0.0 19.2 %copy-start = (bf16[4,2,128,256]{3,2,1,0:T(8,128)(2,1)S(1)}, bf16[4,2,128,256]{3,2,1,0:T(8,128)(2,1)}, u32[]{:S(2)}) copy-start(bf16[4,2,128,256]{3,2,1,0:T(8,128)(2,1)} %slip_ref.5) | copy-start | bytes 1572868
  2.8 25.0 %all-to-all-start = ((bf16[16,32,128]{2,1,0:T(8,128)(2,1)}), bf16[16,32,128]{2,1,0:T(8,128)(2,1)S(1)}, u32[]{:S(2)}, u32[]{:S(2)}) async-start(bf16[16,32,128]{2,1,0:T(8,128)(2,1)} %up.1.after_ref), calls=%async_computation | async-start | bytes 262144 | tf_op jit(solution)/shard_map/all_to_all | solution.py:288
  19.3 19.3 %collective-permute-start.1 = (bf16[2,128,256]{2,1,0:T(8,128)(2,1)S(1)}, bf16[2,128,256]{2,1,0:T(8,128)(2,1)S(1)}, u32[]{:S(2)}, u32[]{:S(2)}) collective-permute-start(bf16[2,128,256]{2,1,0:T(8,128)(2,1)S(1)} %get-tuple-element.10.after_ref), channel_id=1, source_target_pairs={{16,0},{32,16},{48,32},{64,48},{80,64},{96,80},{112,96},{128,112},... | collective-permute-start | bytes 393224 | tf_op jit(solution)/shard_map/ppermute | solution.py:286
  22.4 16.2 %collective-permute-start = (bf16[2,128,256]{2,1,0:T(8,128)(2,1)S(1)}, bf16[2,128,256]{2,1,0:T(8,128)(2,1)S(1)}, u32[]{:S(2)}, u32[]{:S(2)}) collective-permute-start(bf16[2,128,256]{2,1,0:T(8,128)(2,1)S(1)} %get-tuple-element.9), channel_id=1, source_target_pairs={{0,16},{16,32},{32,48},{48,64},{64,80},{80,96},{96,112},{112,128},... | collective-permute-start | bytes 393224 | tf_op jit(solution)/shard_map/ppermute | solution.py:285
  28.5 16.2 %copy-start.4 = (f32[1,16,64,64]{3,2,1,0:T(8,128)S(1)}, f32[1,16,64,64]{3,2,1,0:T(8,128)}, u32[]{:S(2)}) copy-start(f32[1,16,64,64]{3,2,1,0:T(8,128)} %param.21) | copy-start | bytes 786436
  28.5 16.2 %copy-start.5 = (s32[1,16]{1,0:T(1,128)S(1)}, s32[1,16]{1,0:T(1,128)}, u32[]{:S(2)}) copy-start(s32[1,16]{1,0:T(1,128)} %param.20) | copy-start | bytes 196
  28.5 17.4 %all-to-all-start.1 = ((bf16[32,32,128]{2,1,0:T(8,128)(2,1)}), bf16[32,32,128]{2,1,0:T(8,128)(2,1)S(1)}, u32[]{:S(2)}, u32[]{:S(2)}) async-start(bf16[32,32,128]{2,1,0:T(8,128)(2,1)} %sum.1.after_sum_ref), calls=%async_computation.1 | async-start | bytes 524288 | tf_op jit(solution)/shard_map/all_to_all | solution.py:315
  39.4 15.2 %collective-permute-start.3 = (bf16[6,128,256]{2,1,0:T(8,128)(2,1)}, bf16[6,128,256]{2,1,0:T(8,128)(2,1)S(1)}, u32[]{:S(2)}, u32[]{:S(2)}) collective-permute-start(bf16[6,128,256]{2,1,0:T(8,128)(2,1)} %get-tuple-element.12.after_ref), channel_id=1, source_target_pairs={{1,0},{2,1},{3,2},{4,3},{5,4},{6,5},{7,6},{8,7},{9,8},{10,9},{11,1... | collective-permute-start | bytes 1179656 | tf_op jit(solution)/shard_map/ppermute | solution.py:317
  40.7 14.0 %collective-permute-start.2 = (bf16[6,128,256]{2,1,0:T(8,128)(2,1)S(1)}, bf16[6,128,256]{2,1,0:T(8,128)(2,1)S(1)}, u32[]{:S(2)}, u32[]{:S(2)}) collective-permute-start(bf16[6,128,256]{2,1,0:T(8,128)(2,1)S(1)} %get-tuple-element.11), channel_id=1, source_target_pairs={{0,1},{1,2},{2,3},{3,4},{4,5},{5,6},{6,7},{7,8},{8,9},{9,10},{10,1... | collective-permute-start | bytes 1179656 | tf_op jit(solution)/shard_map/ppermute | solution.py:316
  45.9 5.8 %copy-start.6 = (s32[4,2,6]{2,1,0:T(2,128)S(1)}, s32[4,2,6]{2,1,0:T(2,128)}, u32[]{:S(2)}) copy-start(s32[4,2,6]{2,1,0:T(2,128)} %param.12) | copy-start | bytes 580
  46.9 9.0 %all-to-all-start.2 = ((bf16[4,32,128]{2,1,0:T(8,128)(2,1)}), bf16[4,32,128]{2,1,0:T(8,128)(2,1)S(1)}, u32[]{:S(2)}, u32[]{:S(2)}) async-start(bf16[4,32,128]{2,1,0:T(8,128)(2,1)} %couple.1.after_ref), calls=%async_computation.2 | async-start | bytes 65536 | tf_op jit(solution)/shard_map/all_to_all | solution.py:352
  51.8 1.5 %copy-start.1 = (f32[1,4,2,64,64]{4,3,2,1,0:T(8,128)S(1)}, f32[1,4,2,64,64]{4,3,2,1,0:T(8,128)}, u32[]{:S(2)}) copy-start(f32[1,4,2,64,64]{4,3,2,1,0:T(8,128)} %param.19) | copy-start | bytes 393220
  51.8 1.5 %copy-start.2 = (f32[4,2,64,64]{3,2,1,0:T(8,128)S(1)}, f32[4,2,64,64]{3,2,1,0:T(8,128)}, u32[]{:S(2)}) copy-start(f32[4,2,64,64]{3,2,1,0:T(8,128)} %param.17) | copy-start | bytes 393220
  51.8 1.5 %copy-start.3 = (bf16[4,2,64,128]{3,2,1,0:T(8,128)(2,1)S(1)}, bf16[4,2,64,128]{3,2,1,0:T(8,128)(2,1)}, u32[]{:S(2)}) copy-start(bf16[4,2,64,128]{3,2,1,0:T(8,128)(2,1)} %param.15) | copy-start | bytes 393220

commit v3 on v2

--- a/solution.py
+++ b/solution.py
@@ -8,7 +8,7 @@
 F32 = jnp.float32
 BF16 = jnp.bfloat16
 QUARTERS = 4
-COL_FIRST = 11
+COL_ORDER = (11, 0, 1, 2, 3, 4, 5, 6, 7, 15, 14, 13, 12, 10, 9, 8)
 ROW_FIRST = 31
 
 
@@ -57,24 +57,29 @@
 def up_kernel(
     strip_up_ref, leaf_up_ref, basis_ref, slip_ref, out_ref, strip_up, leaf_up, basis, slip, sems
 ):
-    leaves = slip_ref.shape[0]
+    leaves, levels = slip_ref.shape[0], strip_up.shape[0]
+    col = lax.axis_index("col")
     copies = fetch(
-        (strip_up_ref, leaf_up_ref, basis_ref, slip_ref), (strip_up, leaf_up, basis, slip), sems
-    )
-    copies[0].wait()
-    s0, s1, s2, s3 = chain_of(strip_up, lax.axis_index("col"), 4)
-    chain = dot_split(dot_split(s3, s2), dot_split(s1, s0))
-    copies[1].wait()
+        [strip_up_ref.at[level, (col >> level) & 1] for level in range(levels)]
+        + [leaf_up_ref, basis_ref, slip_ref],
+        [strip_up.at[level] for level in range(levels)] + [leaf_up, basis, slip],
+        sems,
+    )
+    for copy in copies[:levels]:
+        copy.wait()
+    chain = dot_split(dot_split(strip_up[3], strip_up[2]), dot_split(strip_up[1], strip_up[0]))
+    copies[levels].wait()
     ups = dot_split(chain, jnp.concatenate([leaf_up[leaf] for leaf in range(leaves)], axis=1))
-    copies[2].wait()
-    copies[3].wait()
+    copies[levels + 1].wait()
+    copies[levels + 2].wait()
     moments = jnp.concatenate([dot(basis[leaf], slip[leaf]) for leaf in range(leaves)], axis=0)
     node = dot_split(ups, moments)
     for quarter in range(QUARTERS):
         half = quarter // 2
         packed = pack(node[:, 128 * half : 128 * (half + 1)], quarter % 2).astype(BF16)
-        for copy in range(out_ref.shape[0] // QUARTERS):
-            out_ref[copy * QUARTERS + (quarter - COL_FIRST) % QUARTERS] = packed
+        for at, place in enumerate(COL_ORDER):
+            if place % QUARTERS == quarter:
+                out_ref[at] = packed
 
 
 def sum_kernel(in_ref, after_ref, out_ref):
@@ -261,7 +266,7 @@
         ups,
         basis,
         slips,
-        scratch=[room(strip_up[0]), room(ups), room(basis), room(slips), dma((4,))],
+        scratch=[room(strip_up[0, :, 0]), room(ups), room(basis), room(slips), dma((strip_up.shape[1] + 3,))],
         name="up",
         flops=100_000_000,
         size=2 * mega,
@@ -284,9 +289,20 @@
     )
     before = lax.ppermute(last, "row", up_row)
     after = lax.ppermute(first, "row", down_row)
-    turned = [(i + COL_FIRST) % n_col for i in range(n_col)]
-    parts = lax.all_to_all(parts, "col", 0, 0, tiled=True, axis_index_groups=[turned])
-    tops = call(sum_kernel, sds((n_row, *piece), BF16), "va", parts, first, name="sum", flops=30_000_000_000, size=mega // 2)
+    weights = call(
+        weights_kernel,
+        sds((4 * rank, n_row * rank // 2), BF16),
+        "sva",
+        strip_lists[0],
+        couplings,
+        first,
+        scratch=[pltpu.VMEM((2 * rank, strips * rank // 2), F32)],
+        name="weights",
+        flops=100_000_000,
+        size=mega,
+    )
+    parts = lax.all_to_all(parts, "col", 0, 0, tiled=True, axis_index_groups=[list(COL_ORDER)])
+    tops = call(sum_kernel, sds((n_row, *piece), BF16), "va", parts, weights, name="sum", flops=30_000_000_000, size=mega // 2)
     rim_left, rim_right = call(
         rim_kernel,
         (sds((along + 2, size, members), BF16), sds((along + 2, size, members), BF16)),
@@ -296,18 +312,6 @@
         after,
         tops,
         name="rim",
-        flops=1_000_000,
-        size=mega,
-    )
-    weights = call(
-        weights_kernel,
-        sds((4 * rank, n_row * rank // 2), BF16),
-        "sva",
-        strip_lists[0],
-        couplings,
-        rim_left,
-        scratch=[pltpu.VMEM((2 * rank, strips * rank // 2), F32)],
-        name="weights",
         flops=30_000_000_000,
         size=mega,
     )

time: 57.5 us -> 55.3 us (0.962)
  starting transfers between devices: 42.8 us -> 41 us
  Pallas kernels: 11.7 us -> 10.8 us
    ppermute x1, starting transfers between devices: 4.01 us -> 1.96 us  [body(): from_left = lax.ppermute(rim_right, 'col', up_col)]
    all_to_all x1, waiting for transfers between devices: 0.01 us -> 1.8 us  [body(): lax.all_to_all(tops, 'row', 0, 0, tiled=True, axis_index_groups=[order])]
    all_to_all x1, waiting for transfers between devices: 2.26 us -> 0.62 us  [body(): lax.all_to_all(parts, 'col', 0, 0, tiled=True, axis_index_groups=[list(CO...]
    pallas_call x10, Pallas kernels: 11.7 us -> 10.8 us  [call(): pl.pallas_call(kernel, out_shape=outs, in_specs=[pl.BlockSpec(memory_spac...]
  transfers between devices with their start and end apart: 7 -> 7, of which waited for: 1 -> 3; matrix products, arithmetic and copies ran while one was open for 0% -> 0% of each run, Pallas kernels for 14% -> 13%
where the time goes in v3:
time: 55.3 us; the launch traced here: 54.8 us
  starting transfers between devices  41 us (74%)
  Pallas kernels  10.8 us (20%)
  waiting for transfers between devices  2.64 us (5%)
    all_to_all x1, starting transfers between devices, body(): lax.all_to_all(parts, 'col', 0, 0, tiled=True, axis_index_groups=[list(CO...  16.4 us
    pallas_call x10, Pallas kernels, call(): pl.pallas_call(kernel, out_shape=outs, in_specs=[pl.BlockSpec(memory_spac...  10.8 us
    all_to_all x1, starting transfers between devices, body(): lax.all_to_all(tops, 'row', 0, 0, tiled=True, axis_index_groups=[order])  10.2 us
    all_to_all x1, starting transfers between devices, body(): lax.all_to_all(coeff, 'col', 0, 0, tiled=True, axis_index_groups=groups)  4.79 us
    ppermute x1, starting transfers between devices, body(): after = lax.ppermute(first, 'row', down_row)  3.28 us
    ppermute x1, starting transfers between devices, body(): before = lax.ppermute(last, 'row', up_row)  3.1 us
    ppermute x1, starting transfers between devices, body(): from_left = lax.ppermute(rim_right, 'col', up_col)  1.96 us
    all_to_all x1, waiting for transfers between devices, body(): lax.all_to_all(tops, 'row', 0, 0, tiled=True, axis_index_groups=[order])  1.8 us
  transfers between devices with their start and end apart: 7, of which 3 were waited for; matrix products, arithmetic and copies ran while one was open for 0% of the time, Pallas kernels for 13%

profile of v3, /device:TPU:1, one launch (start us, length us, event | category | flops | bytes accessed | tf_op | source)
XLA Modules:
  0.0 54.8 jit_solution(15963185755808371266)
XLA Ops:
  0.0 0.0 copy-start
  0.0 2.7 %up.1.after_ref = bf16[16,32,128]{2,1,0:T(8,128)(2,1)} custom-call(f32[4,2,64,64]{3,2,1,0:T(8,128)} %bitcast.16, f32[8,64,64]{2,1,0:T(8,128)} %bitcast.17, bf16[8,64,128]{2,1,0:T(8,128)(2,1)} %bitcast.18, bf16[8,128,256]{2,1,0:T(8,128)(2,1)} %bitcast.10), custom_call_target="tpu_custom_call" | custom-call | flops 100000000 | bytes 2097152 | tf_op jit(solution)/shard_map/up/pallas_call | solution.py:216
  2.7 16.4 %all-to-all-start = ((bf16[16,32,128]{2,1,0:T(8,128)(2,1)}), bf16[16,32,128]{2,1,0:T(8,128)(2,1)S(1)}, u32[]{:S(2)}, u32[]{:S(2)}) async-start(bf16[16,32,128]{2,1,0:T(8,128)(2,1)} %up.1.after_ref), calls=%async_computation | async-start | bytes 262144 | tf_op jit(solution)/shard_map/all_to_all | solution.py:304
  19.1 0.0 copy-done
  19.1 0.0 copy-start.1
  19.1 0.0 copy-start.5
  19.2 3.3 %collective-permute-start.1 = (bf16[2,128,256]{2,1,0:T(8,128)(2,1)S(1)}, bf16[2,128,256]{2,1,0:T(8,128)(2,1)S(1)}, u32[]{:S(2)}, u32[]{:S(2)}) collective-permute-start(bf16[2,128,256]{2,1,0:T(8,128)(2,1)S(1)} %get-tuple-element.10.after_ref), channel_id=1, source_target_pairs={{16,0},{32,16},{48,32},{64,48},{80,64},{96,80},{112,96},{128,112},... | collective-permute-start | bytes 393224 | tf_op jit(solution)/shard_map/ppermute | solution.py:291
  22.4 3.1 %collective-permute-start = (bf16[2,128,256]{2,1,0:T(8,128)(2,1)S(1)}, bf16[2,128,256]{2,1,0:T(8,128)(2,1)S(1)}, u32[]{:S(2)}, u32[]{:S(2)}) collective-permute-start(bf16[2,128,256]{2,1,0:T(8,128)(2,1)S(1)} %get-tuple-element.9), channel_id=1, source_target_pairs={{0,16},{16,32},{32,48},{48,64},{64,80},{80,96},{96,112},{112,128},... | collective-permute-start | bytes 393224 | tf_op jit(solution)/shard_map/ppermute | solution.py:290
  25.6 0.0 copy-done.1
  25.6 0.0 copy-done.5
  25.6 1.2 %weights.1.after_ref.weights_ref = bf16[256,1024]{1,0:T(8,128)(2,1)S(1)} custom-call(s32[16]{0:T(128)S(1)} %bitcast.15, f32[16,64,64]{2,1,0:T(8,128)S(1)} %bitcast.11, bf16[2,128,256]{2,1,0:T(8,128)(2,1)S(1)} %get-tuple-element.10.after_ref), custom_call_target="tpu_custom_call" | custom-call | flops 100000000 | bytes 1048576 | tf_op jit(solution)/shard_map/weights/pallas_call | solution.py:216
  26.8 0.6 %all-to-all-done.in_ref = bf16[16,32,128]{2,1,0:T(8,128)(2,1)S(1)} async-done(((bf16[16,32,128]{2,1,0:T(8,128)(2,1)}), bf16[16,32,128]{2,1,0:T(8,128)(2,1)S(1)}, u32[]{:S(2)}, u32[]{:S(2)}) %all-to-all-start) | async-done | bytes 131104 | tf_op jit(solution)/shard_map/all_to_all | solution.py:304
  27.4 0.7 %sum.1.after_sum_ref = bf16[32,32,128]{2,1,0:T(8,128)(2,1)} custom-call(bf16[16,32,128]{2,1,0:T(8,128)(2,1)S(1)} %all-to-all-done.in_ref, bf16[256,1024]{1,0:T(8,128)(2,1)S(1)} %weights.1.after_ref.weights_ref), custom_call_target="tpu_custom_call" | custom-call | flops 30000001024 | bytes 524288 | tf_op jit(solution)/shard_map/sum/pallas_call | solution.py:216
  28.1 10.2 %all-to-all-start.1 = ((bf16[32,32,128]{2,1,0:T(8,128)(2,1)}), bf16[32,32,128]{2,1,0:T(8,128)(2,1)S(1)}, u32[]{:S(2)}, u32[]{:S(2)}) async-start(bf16[32,32,128]{2,1,0:T(8,128)(2,1)} %sum.1.after_sum_ref), calls=%async_computation.1 | async-start | bytes 524288 | tf_op jit(solution)/shard_map/all_to_all | solution.py:319
  38.3 0.0 collective-permute-done.1.after_ref
  38.3 0.0 collective-permute-done.before_ref
  38.3 0.1 rim.1
  38.4 2.0 %collective-permute-start.2 = (bf16[6,128,256]{2,1,0:T(8,128)(2,1)S(1)}, bf16[6,128,256]{2,1,0:T(8,128)(2,1)S(1)}, u32[]{:S(2)}, u32[]{:S(2)}) collective-permute-start(bf16[6,128,256]{2,1,0:T(8,128)(2,1)S(1)} %get-tuple-element.11), channel_id=1, source_target_pairs={{0,1},{1,2},{2,3},{3,4},{4,5},{5,6},{6,7},{7,8},{8,9},{9,10},{10,1... | collective-permute-start | bytes 1179656 | tf_op jit(solution)/shard_map/ppermute | solution.py:320
  40.4 0.0 copy-start.6
  40.4 1.3 %collective-permute-start.3 = (bf16[6,128,256]{2,1,0:T(8,128)(2,1)S(1)}, bf16[6,128,256]{2,1,0:T(8,128)(2,1)S(1)}, u32[]{:S(2)}, u32[]{:S(2)}) collective-permute-start(bf16[6,128,256]{2,1,0:T(8,128)(2,1)S(1)} %get-tuple-element.12), channel_id=1, source_target_pairs={{1,0},{2,1},{3,2},{4,3},{5,4},{6,5},{7,6},{8,7},{9,8},{10,9},{11,1... | collective-permute-start | bytes 1179656 | tf_op jit(solution)/shard_map/ppermute | solution.py:321
  41.7 1.8 %all-to-all-done.1.tops_ref = bf16[32,32,128]{2,1,0:T(8,128)(2,1)S(1)} async-done(((bf16[32,32,128]{2,1,0:T(8,128)(2,1)}), bf16[32,32,128]{2,1,0:T(8,128)(2,1)S(1)}, u32[]{:S(2)}, u32[]{:S(2)}) %all-to-all-start.1) | async-done | bytes 262176 | tf_op jit(solution)/shard_map/all_to_all | solution.py:319
  43.5 1.0 %couple.1.after_ref = bf16[4,32,128]{2,1,0:T(8,128)(2,1)} custom-call(bf16[32,32,128]{2,1,0:T(8,128)(2,1)S(1)} %all-to-all-done.1.tops_ref, bf16[256,1024]{1,0:T(8,128)(2,1)S(1)} %weights.1.after_ref.weights_ref), custom_call_target="tpu_custom_call" | custom-call | flops 30000001024 | bytes 524288 | tf_op jit(solution)/shard_map/couple/pallas_call | solution.py:216
  44.5 4.8 %all-to-all-start.2 = ((bf16[4,32,128]{2,1,0:T(8,128)(2,1)}), bf16[4,32,128]{2,1,0:T(8,128)(2,1)S(1)}, u32[]{:S(2)}, u32[]{:S(2)}) async-start(bf16[4,32,128]{2,1,0:T(8,128)(2,1)} %couple.1.after_ref), calls=%async_computation.2 | async-start | bytes 65536 | tf_op jit(solution)/shard_map/all_to_all | solution.py:356
  49.2 0.0 copy-done.6
  49.3 0.1 reshape.21.lists_ref
  49.3 0.0 copy-start.2
  49.3 0.0 copy-start.3
  49.3 0.0 copy-start.4
  49.4 1.5 %hold.1.blocks_ref = bf16[4,2,6,128,128]{4,3,2,1,0:T(8,128)(2,1)S(1)} custom-call(bf16[4,2,6,128,128]{4,3,2,1,0:T(8,128)(2,1)} %blocks_ref.1, bf16[4,32,128]{2,1,0:T(8,128)(2,1)} %couple.1.after_ref), custom_call_target="tpu_custom_call" | custom-call | flops 1000000 | bytes 2097152 | tf_op jit(solution)/shard_map/hold/pallas_call | solution.py:216
  50.8 0.0 copy-done.2
  50.9 0.0 copy-done.3
  50.9 0.0 copy-done.4
  50.9 1.3 %far.1.far_ref = bf16[1024,128]{1,0:T(8,128)(2,1)S(1)} custom-call(f32[4,2,64,64]{3,2,1,0:T(8,128)S(1)} %bitcast.12, f32[8,64,64]{2,1,0:T(8,128)S(1)} %bitcast.13, bf16[8,64,128]{2,1,0:T(8,128)(2,1)S(1)} %bitcast.14, bf16[4,32,128]{2,1,0:T(8,128)(2,1)} %couple.1.after_ref), custom_call_target="tpu_custom_call" | custom-call | flops 100000000 | bytes 1048576 | tf_op jit(solution)/shard_map/far/pallas_call | solution.py:216
  52.2 0.0 collective-permute-done.2.left_ref
  52.2 0.0 collective-permute-done.3.right_ref
  52.2 1.3 %near.1.near_ref = f32[8,128,256]{2,1,0:T(8,128)S(1)} custom-call(s32[48]{0:T(128)S(1)} %reshape.21.lists_ref, bf16[4,2,128,256]{3,2,1,0:T(8,128)(2,1)S(1)} %copy-done, bf16[2,128,256]{2,1,0:T(8,128)(2,1)S(1)} %collective-permute-done.before_ref, bf16[2,128,256]{2,1,0:T(8,128)(2,1)S(1)} %collective-permute-done.1.after_ref, ...), custom_call_target="tpu_custom_call" | custom-call | flops 402653184 | bytes 4194304 | tf_op jit(solution)/shard_map/near/pallas_call | solution.py:216
  53.5 0.2 all-to-all-done.2.coeff_ref
  53.7 1.1 %final.1 = bf16[8,128,256]{2,1,0:T(8,128)(2,1)} custom-call(f32[8,128,256]{2,1,0:T(8,128)S(1)} %near.1.near_ref, bf16[1024,128]{1,0:T(8,128)(2,1)S(1)} %far.1.far_ref, bf16[4,32,128]{2,1,0:T(8,128)(2,1)S(1)} %all-to-all-done.2.coeff_ref), custom_call_target="tpu_custom_call" | custom-call | flops 67108864 | bytes 2097152 | tf_op jit(solution)/shard_map/final/pallas_call | solution.py:216
  (1 shorter events, 0.0 us)
Async XLA Ops:
  0.0 19.1 %copy-start = (bf16[4,2,128,256]{3,2,1,0:T(8,128)(2,1)S(1)}, bf16[4,2,128,256]{3,2,1,0:T(8,128)(2,1)}, u32[]{:S(2)}) copy-start(bf16[4,2,128,256]{3,2,1,0:T(8,128)(2,1)} %slip_ref.5) | copy-start | bytes 1572868
  2.7 24.7 %all-to-all-start = ((bf16[16,32,128]{2,1,0:T(8,128)(2,1)}), bf16[16,32,128]{2,1,0:T(8,128)(2,1)S(1)}, u32[]{:S(2)}, u32[]{:S(2)}) async-start(bf16[16,32,128]{2,1,0:T(8,128)(2,1)} %up.1.after_ref), calls=%async_computation | async-start | bytes 262144 | tf_op jit(solution)/shard_map/all_to_all | solution.py:304
  19.1 6.4 %copy-start.1 = (f32[1,16,64,64]{3,2,1,0:T(8,128)S(1)}, f32[1,16,64,64]{3,2,1,0:T(8,128)}, u32[]{:S(2)}) copy-start(f32[1,16,64,64]{3,2,1,0:T(8,128)} %param.21) | copy-start | bytes 786436
  19.1 6.4 %copy-start.5 = (s32[1,16]{1,0:T(1,128)S(1)}, s32[1,16]{1,0:T(1,128)}, u32[]{:S(2)}) copy-start(s32[1,16]{1,0:T(1,128)} %param.20) | copy-start | bytes 196
  19.2 19.2 %collective-permute-start.1 = (bf16[2,128,256]{2,1,0:T(8,128)(2,1)S(1)}, bf16[2,128,256]{2,1,0:T(8,128)(2,1)S(1)}, u32[]{:S(2)}, u32[]{:S(2)}) collective-permute-start(bf16[2,128,256]{2,1,0:T(8,128)(2,1)S(1)} %get-tuple-element.10.after_ref), channel_id=1, source_target_pairs={{16,0},{32,16},{48,32},{64,48},{80,64},{96,80},{112,96},{128,112},... | collective-permute-start | bytes 393224 | tf_op jit(solution)/shard_map/ppermute | solution.py:291
  22.4 15.9 %collective-permute-start = (bf16[2,128,256]{2,1,0:T(8,128)(2,1)S(1)}, bf16[2,128,256]{2,1,0:T(8,128)(2,1)S(1)}, u32[]{:S(2)}, u32[]{:S(2)}) collective-permute-start(bf16[2,128,256]{2,1,0:T(8,128)(2,1)S(1)} %get-tuple-element.9), channel_id=1, source_target_pairs={{0,16},{16,32},{32,48},{48,64},{64,80},{80,96},{96,112},{112,128},... | collective-permute-start | bytes 393224 | tf_op jit(solution)/shard_map/ppermute | solution.py:290
  28.1 15.4 %all-to-all-start.1 = ((bf16[32,32,128]{2,1,0:T(8,128)(2,1)}), bf16[32,32,128]{2,1,0:T(8,128)(2,1)S(1)}, u32[]{:S(2)}, u32[]{:S(2)}) async-start(bf16[32,32,128]{2,1,0:T(8,128)(2,1)} %sum.1.after_sum_ref), calls=%async_computation.1 | async-start | bytes 524288 | tf_op jit(solution)/shard_map/all_to_all | solution.py:319
  38.4 13.8 %collective-permute-start.2 = (bf16[6,128,256]{2,1,0:T(8,128)(2,1)S(1)}, bf16[6,128,256]{2,1,0:T(8,128)(2,1)S(1)}, u32[]{:S(2)}, u32[]{:S(2)}) collective-permute-start(bf16[6,128,256]{2,1,0:T(8,128)(2,1)S(1)} %get-tuple-element.11), channel_id=1, source_target_pairs={{0,1},{1,2},{2,3},{3,4},{4,5},{5,6},{6,7},{7,8},{8,9},{9,10},{10,1... | collective-permute-start | bytes 1179656 | tf_op jit(solution)/shard_map/ppermute | solution.py:320
  40.4 8.9 %copy-start.6 = (s32[4,2,6]{2,1,0:T(2,128)S(1)}, s32[4,2,6]{2,1,0:T(2,128)}, u32[]{:S(2)}) copy-start(s32[4,2,6]{2,1,0:T(2,128)} %param.12) | copy-start | bytes 580
  40.4 11.8 %collective-permute-start.3 = (bf16[6,128,256]{2,1,0:T(8,128)(2,1)S(1)}, bf16[6,128,256]{2,1,0:T(8,128)(2,1)S(1)}, u32[]{:S(2)}, u32[]{:S(2)}) collective-permute-start(bf16[6,128,256]{2,1,0:T(8,128)(2,1)S(1)} %get-tuple-element.12), channel_id=1, source_target_pairs={{1,0},{2,1},{3,2},{4,3},{5,4},{6,5},{7,6},{8,7},{9,8},{10,9},{11,1... | collective-permute-start | bytes 1179656 | tf_op jit(solution)/shard_map/ppermute | solution.py:321
  44.5 9.2 %all-to-all-start.2 = ((bf16[4,32,128]{2,1,0:T(8,128)(2,1)}), bf16[4,32,128]{2,1,0:T(8,128)(2,1)S(1)}, u32[]{:S(2)}, u32[]{:S(2)}) async-start(bf16[4,32,128]{2,1,0:T(8,128)(2,1)} %couple.1.after_ref), calls=%async_computation.2 | async-start | bytes 65536 | tf_op jit(solution)/shard_map/all_to_all | solution.py:356
  49.3 1.5 %copy-start.2 = (f32[1,4,2,64,64]{4,3,2,1,0:T(8,128)S(1)}, f32[1,4,2,64,64]{4,3,2,1,0:T(8,128)}, u32[]{:S(2)}) copy-start(f32[1,4,2,64,64]{4,3,2,1,0:T(8,128)} %param.19) | copy-start | bytes 393220
  49.3 1.5 %copy-start.3 = (f32[4,2,64,64]{3,2,1,0:T(8,128)S(1)}, f32[4,2,64,64]{3,2,1,0:T(8,128)}, u32[]{:S(2)}) copy-start(f32[4,2,64,64]{3,2,1,0:T(8,128)} %param.17) | copy-start | bytes 393220
  49.3 1.5 %copy-start.4 = (bf16[4,2,64,128]{3,2,1,0:T(8,128)(2,1)S(1)}, bf16[4,2,64,128]{3,2,1,0:T(8,128)(2,1)}, u32[]{:S(2)}) copy-start(bf16[4,2,64,128]{3,2,1,0:T(8,128)(2,1)} %param.15) | copy-start | bytes 393220

commit v4 on v3

--- a/solution.py
+++ b/solution.py
@@ -9,7 +9,8 @@
 BF16 = jnp.bfloat16
 QUARTERS = 4
 COL_ORDER = (11, 0, 1, 2, 3, 4, 5, 6, 7, 15, 14, 13, 12, 10, 9, 8)
-ROW_FIRST = 31
+ROW_FIRST = 21
+GROUP_ORDER = (2, 3, 1, 0)
 
 
 def halves(value):
@@ -192,8 +193,8 @@
     left = lax.broadcasted_iota(jnp.int32, (rows, lanes), 1) < lanes // 2
     tiles = []
     for half in range(2):
-        one = coeff_ref[QUARTERS - 1 - 2 * half].astype(F32)
-        two = coeff_ref[QUARTERS - 2 - 2 * half].astype(F32)
+        one = coeff_ref[GROUP_ORDER.index(2 * half)].astype(F32)
+        two = coeff_ref[GROUP_ORDER.index(2 * half + 1)].astype(F32)
         upper = jnp.where(left, one, pltpu.roll(two, lanes // 2, 1))
         lower = jnp.where(left, pltpu.roll(one, lanes // 2, 1), two)
         tiles.append(jnp.concatenate([upper, lower], axis=0).astype(BF16))
@@ -352,7 +353,7 @@
         flops=1_000_000,
         size=2 * mega,
     )
-    groups = [list(range(i, i + QUARTERS))[::-1] for i in range(0, n_col, QUARTERS)]
+    groups = [[i + at for at in GROUP_ORDER] for i in range(0, n_col, QUARTERS)]
     coeff = lax.all_to_all(coeff, "col", 0, 0, tiled=True, axis_index_groups=groups)
     near = call(
         near_kernel,

time: 55.3 us -> 55.6 us (level)
    all_to_all x1, waiting for transfers between devices: 1.8 us -> 0.75 us  [body(): lax.all_to_all(tops, 'row', 0, 0, tiled=True, axis_index_groups=[order])]
    ppermute x1, waiting for transfers between devices: 0.05 us -> 0.99 us  [body(): from_right = lax.ppermute(rim_left, 'col', down_col)]
  transfers between devices with their start and end apart: 7 -> 7, of which waited for: 3 -> 4; matrix products, arithmetic and copies ran while one was open for 0% -> 0% of each run, Pallas kernels for 13% -> 13%
where the time goes in v4:
time: 55.6 us; the launch traced here: 55.1 us
  starting transfers between devices  41.4 us (74%)
  Pallas kernels  10.8 us (19%)
  waiting for transfers between devices  2.66 us (5%)
    all_to_all x1, starting transfers between devices, body(): lax.all_to_all(parts, 'col', 0, 0, tiled=True, axis_index_groups=[list(CO...  16.4 us
    pallas_call x10, Pallas kernels, call(): pl.pallas_call(kernel, out_shape=outs, in_specs=[pl.BlockSpec(memory_spac...  10.8 us
    all_to_all x1, starting transfers between devices, body(): lax.all_to_all(tops, 'row', 0, 0, tiled=True, axis_index_groups=[order])  10.4 us
    all_to_all x1, starting transfers between devices, body(): lax.all_to_all(coeff, 'col', 0, 0, tiled=True, axis_index_groups=groups)  4.9 us
    ppermute x1, starting transfers between devices, body(): after = lax.ppermute(first, 'row', down_row)  3.28 us
    ppermute x1, starting transfers between devices, body(): before = lax.ppermute(last, 'row', up_row)  3.1 us
    ppermute x1, starting transfers between devices, body(): from_left = lax.ppermute(rim_right, 'col', up_col)  1.96 us
    ppermute x1, starting transfers between devices, body(): from_right = lax.ppermute(rim_left, 'col', down_col)  1.29 us
  transfers between devices with their start and end apart: 7, of which 4 were waited for; matrix products, arithmetic and copies ran while one was open for 0% of the time, Pallas kernels for 13%

profile of v4, /device:TPU:1, one launch (start us, length us, event | category | flops | bytes accessed | tf_op | source)
XLA Modules:
  0.0 55.1 jit_solution(9004876735472975210)
XLA Ops:
  0.0 0.0 copy-start
  0.0 2.7 %up.1.after_ref = bf16[16,32,128]{2,1,0:T(8,128)(2,1)} custom-call(f32[4,2,64,64]{3,2,1,0:T(8,128)} %bitcast.16, f32[8,64,64]{2,1,0:T(8,128)} %bitcast.17, bf16[8,64,128]{2,1,0:T(8,128)(2,1)} %bitcast.18, bf16[8,128,256]{2,1,0:T(8,128)(2,1)} %bitcast.10), custom_call_target="tpu_custom_call" | custom-call | flops 100000000 | bytes 2097152 | tf_op jit(solution)/shard_map/up/pallas_call | solution.py:217
  2.7 16.4 %all-to-all-start = ((bf16[16,32,128]{2,1,0:T(8,128)(2,1)}), bf16[16,32,128]{2,1,0:T(8,128)(2,1)S(1)}, u32[]{:S(2)}, u32[]{:S(2)}) async-start(bf16[16,32,128]{2,1,0:T(8,128)(2,1)} %up.1.after_ref), calls=%async_computation | async-start | bytes 262144 | tf_op jit(solution)/shard_map/all_to_all | solution.py:305
  19.1 0.0 copy-done
  19.1 0.0 copy-start.1
  19.1 0.0 copy-start.5
  19.2 3.3 %collective-permute-start.1 = (bf16[2,128,256]{2,1,0:T(8,128)(2,1)S(1)}, bf16[2,128,256]{2,1,0:T(8,128)(2,1)S(1)}, u32[]{:S(2)}, u32[]{:S(2)}) collective-permute-start(bf16[2,128,256]{2,1,0:T(8,128)(2,1)S(1)} %get-tuple-element.10.after_ref), channel_id=1, source_target_pairs={{16,0},{32,16},{48,32},{64,48},{80,64},{96,80},{112,96},{128,112},... | collective-permute-start | bytes 393224 | tf_op jit(solution)/shard_map/ppermute | solution.py:292
  22.4 3.1 %collective-permute-start = (bf16[2,128,256]{2,1,0:T(8,128)(2,1)S(1)}, bf16[2,128,256]{2,1,0:T(8,128)(2,1)S(1)}, u32[]{:S(2)}, u32[]{:S(2)}) collective-permute-start(bf16[2,128,256]{2,1,0:T(8,128)(2,1)S(1)} %get-tuple-element.9), channel_id=1, source_target_pairs={{0,16},{16,32},{32,48},{48,64},{64,80},{80,96},{96,112},{112,128},... | collective-permute-start | bytes 393224 | tf_op jit(solution)/shard_map/ppermute | solution.py:291
  25.6 0.0 copy-done.1
  25.6 0.0 copy-done.5
  25.6 1.2 %weights.1.after_ref.weights_ref = bf16[256,1024]{1,0:T(8,128)(2,1)S(1)} custom-call(s32[16]{0:T(128)S(1)} %bitcast.15, f32[16,64,64]{2,1,0:T(8,128)S(1)} %bitcast.11, bf16[2,128,256]{2,1,0:T(8,128)(2,1)S(1)} %get-tuple-element.10.after_ref), custom_call_target="tpu_custom_call" | custom-call | flops 100000000 | bytes 1048576 | tf_op jit(solution)/shard_map/weights/pallas_call | solution.py:217
  26.8 0.6 %all-to-all-done.in_ref = bf16[16,32,128]{2,1,0:T(8,128)(2,1)S(1)} async-done(((bf16[16,32,128]{2,1,0:T(8,128)(2,1)}), bf16[16,32,128]{2,1,0:T(8,128)(2,1)S(1)}, u32[]{:S(2)}, u32[]{:S(2)}) %all-to-all-start) | async-done | bytes 131104 | tf_op jit(solution)/shard_map/all_to_all | solution.py:305
  27.4 0.7 %sum.1.after_sum_ref = bf16[32,32,128]{2,1,0:T(8,128)(2,1)} custom-call(bf16[16,32,128]{2,1,0:T(8,128)(2,1)S(1)} %all-to-all-done.in_ref, bf16[256,1024]{1,0:T(8,128)(2,1)S(1)} %weights.1.after_ref.weights_ref), custom_call_target="tpu_custom_call" | custom-call | flops 30000001024 | bytes 524288 | tf_op jit(solution)/shard_map/sum/pallas_call | solution.py:217
  28.1 10.4 %all-to-all-start.1 = ((bf16[32,32,128]{2,1,0:T(8,128)(2,1)}), bf16[32,32,128]{2,1,0:T(8,128)(2,1)S(1)}, u32[]{:S(2)}, u32[]{:S(2)}) async-start(bf16[32,32,128]{2,1,0:T(8,128)(2,1)} %sum.1.after_sum_ref), calls=%async_computation.1 | async-start | bytes 524288 | tf_op jit(solution)/shard_map/all_to_all | solution.py:320
  38.5 0.0 collective-permute-done.1.after_ref
  38.6 0.0 collective-permute-done.before_ref
  38.6 0.1 rim.1
  38.6 2.0 %collective-permute-start.2 = (bf16[6,128,256]{2,1,0:T(8,128)(2,1)S(1)}, bf16[6,128,256]{2,1,0:T(8,128)(2,1)S(1)}, u32[]{:S(2)}, u32[]{:S(2)}) collective-permute-start(bf16[6,128,256]{2,1,0:T(8,128)(2,1)S(1)} %get-tuple-element.11), channel_id=1, source_target_pairs={{0,1},{1,2},{2,3},{3,4},{4,5},{5,6},{6,7},{7,8},{8,9},{9,10},{10,1... | collective-permute-start | bytes 1179656 | tf_op jit(solution)/shard_map/ppermute | solution.py:321
  40.6 0.0 copy-start.6
  40.6 1.3 %collective-permute-start.3 = (bf16[6,128,256]{2,1,0:T(8,128)(2,1)S(1)}, bf16[6,128,256]{2,1,0:T(8,128)(2,1)S(1)}, u32[]{:S(2)}, u32[]{:S(2)}) collective-permute-start(bf16[6,128,256]{2,1,0:T(8,128)(2,1)S(1)} %get-tuple-element.12), channel_id=1, source_target_pairs={{1,0},{2,1},{3,2},{4,3},{5,4},{6,5},{7,6},{8,7},{9,8},{10,9},{11,1... | collective-permute-start | bytes 1179656 | tf_op jit(solution)/shard_map/ppermute | solution.py:322
  41.9 0.8 %all-to-all-done.1.tops_ref = bf16[32,32,128]{2,1,0:T(8,128)(2,1)S(1)} async-done(((bf16[32,32,128]{2,1,0:T(8,128)(2,1)}), bf16[32,32,128]{2,1,0:T(8,128)(2,1)S(1)}, u32[]{:S(2)}, u32[]{:S(2)}) %all-to-all-start.1) | async-done | bytes 262176 | tf_op jit(solution)/shard_map/all_to_all | solution.py:320
  42.7 1.0 %couple.1.after_ref = bf16[4,32,128]{2,1,0:T(8,128)(2,1)} custom-call(bf16[32,32,128]{2,1,0:T(8,128)(2,1)S(1)} %all-to-all-done.1.tops_ref, bf16[256,1024]{1,0:T(8,128)(2,1)S(1)} %weights.1.after_ref.weights_ref), custom_call_target="tpu_custom_call" | custom-call | flops 30000001024 | bytes 524288 | tf_op jit(solution)/shard_map/couple/pallas_call | solution.py:217
  43.6 4.9 %all-to-all-start.2 = ((bf16[4,32,128]{2,1,0:T(8,128)(2,1)}), bf16[4,32,128]{2,1,0:T(8,128)(2,1)S(1)}, u32[]{:S(2)}, u32[]{:S(2)}) async-start(bf16[4,32,128]{2,1,0:T(8,128)(2,1)} %couple.1.after_ref), calls=%async_computation.2 | async-start | bytes 65536 | tf_op jit(solution)/shard_map/all_to_all | solution.py:357
  48.5 0.0 copy-done.6
  48.5 0.1 reshape.21.lists_ref
  48.6 0.0 copy-start.2
  48.6 0.0 copy-start.3
  48.6 0.0 copy-start.4
  48.6 1.5 %hold.1.blocks_ref = bf16[4,2,6,128,128]{4,3,2,1,0:T(8,128)(2,1)S(1)} custom-call(bf16[4,2,6,128,128]{4,3,2,1,0:T(8,128)(2,1)} %blocks_ref.1, bf16[4,32,128]{2,1,0:T(8,128)(2,1)} %couple.1.after_ref), custom_call_target="tpu_custom_call" | custom-call | flops 1000000 | bytes 2097152 | tf_op jit(solution)/shard_map/hold/pallas_call | solution.py:217
  50.1 0.0 copy-done.2
  50.1 0.0 copy-done.3
  50.1 0.0 copy-done.4
  50.2 1.3 %far.1.far_ref = bf16[1024,128]{1,0:T(8,128)(2,1)S(1)} custom-call(f32[4,2,64,64]{3,2,1,0:T(8,128)S(1)} %bitcast.12, f32[8,64,64]{2,1,0:T(8,128)S(1)} %bitcast.13, bf16[8,64,128]{2,1,0:T(8,128)(2,1)S(1)} %bitcast.14, bf16[4,32,128]{2,1,0:T(8,128)(2,1)} %couple.1.after_ref), custom_call_target="tpu_custom_call" | custom-call | flops 100000000 | bytes 1048576 | tf_op jit(solution)/shard_map/far/pallas_call | solution.py:217
  51.4 0.0 collective-permute-done.2.left_ref
  51.5 1.0 %collective-permute-done.3.right_ref = bf16[6,128,256]{2,1,0:T(8,128)(2,1)S(1)} collective-permute-done((bf16[6,128,256]{2,1,0:T(8,128)(2,1)S(1)}, bf16[6,128,256]{2,1,0:T(8,128)(2,1)S(1)}, u32[]{:S(2)}, u32[]{:S(2)}) %collective-permute-start.3) | collective-permute-done | bytes 393248 | tf_op jit(solution)/shard_map/ppermute | solution.py:322
  52.4 1.3 %near.1.near_ref = f32[8,128,256]{2,1,0:T(8,128)S(1)} custom-call(s32[48]{0:T(128)S(1)} %reshape.21.lists_ref, bf16[4,2,128,256]{3,2,1,0:T(8,128)(2,1)S(1)} %copy-done, bf16[2,128,256]{2,1,0:T(8,128)(2,1)S(1)} %collective-permute-done.before_ref, bf16[2,128,256]{2,1,0:T(8,128)(2,1)S(1)} %collective-permute-done.1.after_ref, ...), custom_call_target="tpu_custom_call" | custom-call | flops 402653184 | bytes 4194304 | tf_op jit(solution)/shard_map/near/pallas_call | solution.py:217
  53.7 0.3 all-to-all-done.2.coeff_ref
  54.0 1.1 %final.1 = bf16[8,128,256]{2,1,0:T(8,128)(2,1)} custom-call(f32[8,128,256]{2,1,0:T(8,128)S(1)} %near.1.near_ref, bf16[1024,128]{1,0:T(8,128)(2,1)S(1)} %far.1.far_ref, bf16[4,32,128]{2,1,0:T(8,128)(2,1)S(1)} %all-to-all-done.2.coeff_ref), custom_call_target="tpu_custom_call" | custom-call | flops 67108864 | bytes 2097152 | tf_op jit(solution)/shard_map/final/pallas_call | solution.py:217
  (1 shorter events, 0.0 us)
Async XLA Ops:
  0.0 19.1 %copy-start = (bf16[4,2,128,256]{3,2,1,0:T(8,128)(2,1)S(1)}, bf16[4,2,128,256]{3,2,1,0:T(8,128)(2,1)}, u32[]{:S(2)}) copy-start(bf16[4,2,128,256]{3,2,1,0:T(8,128)(2,1)} %slip_ref.5) | copy-start | bytes 1572868
  2.7 24.7 %all-to-all-start = ((bf16[16,32,128]{2,1,0:T(8,128)(2,1)}), bf16[16,32,128]{2,1,0:T(8,128)(2,1)S(1)}, u32[]{:S(2)}, u32[]{:S(2)}) async-start(bf16[16,32,128]{2,1,0:T(8,128)(2,1)} %up.1.after_ref), calls=%async_computation | async-start | bytes 262144 | tf_op jit(solution)/shard_map/all_to_all | solution.py:305
  19.1 6.4 %copy-start.1 = (f32[1,16,64,64]{3,2,1,0:T(8,128)S(1)}, f32[1,16,64,64]{3,2,1,0:T(8,128)}, u32[]{:S(2)}) copy-start(f32[1,16,64,64]{3,2,1,0:T(8,128)} %param.21) | copy-start | bytes 786436
  19.1 6.4 %copy-start.5 = (s32[1,16]{1,0:T(1,128)S(1)}, s32[1,16]{1,0:T(1,128)}, u32[]{:S(2)}) copy-start(s32[1,16]{1,0:T(1,128)} %param.20) | copy-start | bytes 196
  19.2 19.4 %collective-permute-start.1 = (bf16[2,128,256]{2,1,0:T(8,128)(2,1)S(1)}, bf16[2,128,256]{2,1,0:T(8,128)(2,1)S(1)}, u32[]{:S(2)}, u32[]{:S(2)}) collective-permute-start(bf16[2,128,256]{2,1,0:T(8,128)(2,1)S(1)} %get-tuple-element.10.after_ref), channel_id=1, source_target_pairs={{16,0},{32,16},{48,32},{64,48},{80,64},{96,80},{112,96},{128,112},... | collective-permute-start | bytes 393224 | tf_op jit(solution)/shard_map/ppermute | solution.py:292
  22.4 16.1 %collective-permute-start = (bf16[2,128,256]{2,1,0:T(8,128)(2,1)S(1)}, bf16[2,128,256]{2,1,0:T(8,128)(2,1)S(1)}, u32[]{:S(2)}, u32[]{:S(2)}) collective-permute-start(bf16[2,128,256]{2,1,0:T(8,128)(2,1)S(1)} %get-tuple-element.9), channel_id=1, source_target_pairs={{0,16},{16,32},{32,48},{48,64},{64,80},{80,96},{96,112},{112,128},... | collective-permute-start | bytes 393224 | tf_op jit(solution)/shard_map/ppermute | solution.py:291
  28.1 14.5 %all-to-all-start.1 = ((bf16[32,32,128]{2,1,0:T(8,128)(2,1)}), bf16[32,32,128]{2,1,0:T(8,128)(2,1)S(1)}, u32[]{:S(2)}, u32[]{:S(2)}) async-start(bf16[32,32,128]{2,1,0:T(8,128)(2,1)} %sum.1.after_sum_ref), calls=%async_computation.1 | async-start | bytes 524288 | tf_op jit(solution)/shard_map/all_to_all | solution.py:320
  38.6 12.8 %collective-permute-start.2 = (bf16[6,128,256]{2,1,0:T(8,128)(2,1)S(1)}, bf16[6,128,256]{2,1,0:T(8,128)(2,1)S(1)}, u32[]{:S(2)}, u32[]{:S(2)}) collective-permute-start(bf16[6,128,256]{2,1,0:T(8,128)(2,1)S(1)} %get-tuple-element.11), channel_id=1, source_target_pairs={{0,1},{1,2},{2,3},{3,4},{4,5},{5,6},{6,7},{7,8},{8,9},{9,10},{10,1... | collective-permute-start | bytes 1179656 | tf_op jit(solution)/shard_map/ppermute | solution.py:321
  40.6 7.9 %copy-start.6 = (s32[4,2,6]{2,1,0:T(2,128)S(1)}, s32[4,2,6]{2,1,0:T(2,128)}, u32[]{:S(2)}) copy-start(s32[4,2,6]{2,1,0:T(2,128)} %param.12) | copy-start | bytes 580
  40.6 11.8 %collective-permute-start.3 = (bf16[6,128,256]{2,1,0:T(8,128)(2,1)S(1)}, bf16[6,128,256]{2,1,0:T(8,128)(2,1)S(1)}, u32[]{:S(2)}, u32[]{:S(2)}) collective-permute-start(bf16[6,128,256]{2,1,0:T(8,128)(2,1)S(1)} %get-tuple-element.12), channel_id=1, source_target_pairs={{1,0},{2,1},{3,2},{4,3},{5,4},{6,5},{7,6},{8,7},{9,8},{10,9},{11,1... | collective-permute-start | bytes 1179656 | tf_op jit(solution)/shard_map/ppermute | solution.py:322
  43.6 10.4 %all-to-all-start.2 = ((bf16[4,32,128]{2,1,0:T(8,128)(2,1)}), bf16[4,32,128]{2,1,0:T(8,128)(2,1)S(1)}, u32[]{:S(2)}, u32[]{:S(2)}) async-start(bf16[4,32,128]{2,1,0:T(8,128)(2,1)} %couple.1.after_ref), calls=%async_computation.2 | async-start | bytes 65536 | tf_op jit(solution)/shard_map/all_to_all | solution.py:357
  48.6 1.5 %copy-start.2 = (f32[1,4,2,64,64]{4,3,2,1,0:T(8,128)S(1)}, f32[1,4,2,64,64]{4,3,2,1,0:T(8,128)}, u32[]{:S(2)}) copy-start(f32[1,4,2,64,64]{4,3,2,1,0:T(8,128)} %param.19) | copy-start | bytes 393220
  48.6 1.5 %copy-start.3 = (f32[4,2,64,64]{3,2,1,0:T(8,128)S(1)}, f32[4,2,64,64]{3,2,1,0:T(8,128)}, u32[]{:S(2)}) copy-start(f32[4,2,64,64]{3,2,1,0:T(8,128)} %param.17) | copy-start | bytes 393220
  48.6 1.5 %copy-start.4 = (bf16[4,2,64,128]{3,2,1,0:T(8,128)(2,1)S(1)}, bf16[4,2,64,128]{3,2,1,0:T(8,128)(2,1)}, u32[]{:S(2)}) copy-start(bf16[4,2,64,128]{3,2,1,0:T(8,128)(2,1)} %param.15) | copy-start | bytes 393220

commit v5 on v3

--- a/solution.py
+++ b/solution.py
@@ -65,13 +65,10 @@
         [strip_up.at[level] for level in range(levels)] + [leaf_up, basis, slip],
         sems,
     )
-    for copy in copies[:levels]:
+    for copy in copies:
         copy.wait()
     chain = dot_split(dot_split(strip_up[3], strip_up[2]), dot_split(strip_up[1], strip_up[0]))
-    copies[levels].wait()
     ups = dot_split(chain, jnp.concatenate([leaf_up[leaf] for leaf in range(leaves)], axis=1))
-    copies[levels + 1].wait()
-    copies[levels + 2].wait()
     moments = jnp.concatenate([dot(basis[leaf], slip[leaf]) for leaf in range(leaves)], axis=0)
     node = dot_split(ups, moments)
     for quarter in range(QUARTERS):

time: 55.3 us -> 55.5 us (level)
  no operation moved by 1% of the time
where the time goes in v5:
time: 55.5 us; the launch traced here: 55 us
  starting transfers between devices  41 us (74%)
  Pallas kernels  11 us (20%)
  waiting for transfers between devices  2.63 us (5%)
    all_to_all x1, starting transfers between devices, body(): lax.all_to_all(parts, 'col', 0, 0, tiled=True, axis_index_groups=[list(CO...  16.4 us
    pallas_call x10, Pallas kernels, call(): pl.pallas_call(kernel, out_shape=outs, in_specs=[pl.BlockSpec(memory_spac...  11 us
    all_to_all x1, starting transfers between devices, body(): lax.all_to_all(tops, 'row', 0, 0, tiled=True, axis_index_groups=[order])  10.2 us
    all_to_all x1, starting transfers between devices, body(): lax.all_to_all(coeff, 'col', 0, 0, tiled=True, axis_index_groups=groups)  4.79 us
    ppermute x1, starting transfers between devices, body(): after = lax.ppermute(first, 'row', down_row)  3.27 us
    ppermute x1, starting transfers between devices, body(): before = lax.ppermute(last, 'row', up_row)  3.1 us
    ppermute x1, starting transfers between devices, body(): from_left = lax.ppermute(rim_right, 'col', up_col)  1.96 us
    all_to_all x1, waiting for transfers between devices, body(): lax.all_to_all(tops, 'row', 0, 0, tiled=True, axis_index_groups=[order])  1.8 us
  transfers between devices with their start and end apart: 7, of which 3 were waited for; matrix products, arithmetic and copies ran while one was open for 0% of the time, Pallas kernels for 13%

profile of v5, /device:TPU:1, one launch (start us, length us, event | category | flops | bytes accessed | tf_op | source)
XLA Modules:
  0.0 55.0 jit_solution(14521455936838845044)
XLA Ops:
  0.0 0.0 copy-start
  0.0 2.9 %up.1.after_ref = bf16[16,32,128]{2,1,0:T(8,128)(2,1)} custom-call(f32[4,2,64,64]{3,2,1,0:T(8,128)} %bitcast.16, f32[8,64,64]{2,1,0:T(8,128)} %bitcast.17, bf16[8,64,128]{2,1,0:T(8,128)(2,1)} %bitcast.18, bf16[8,128,256]{2,1,0:T(8,128)(2,1)} %bitcast.10), custom_call_target="tpu_custom_call" | custom-call | flops 100000000 | bytes 2097152 | tf_op jit(solution)/shard_map/up/pallas_call | solution.py:213
  2.9 16.4 %all-to-all-start = ((bf16[16,32,128]{2,1,0:T(8,128)(2,1)}), bf16[16,32,128]{2,1,0:T(8,128)(2,1)S(1)}, u32[]{:S(2)}, u32[]{:S(2)}) async-start(bf16[16,32,128]{2,1,0:T(8,128)(2,1)} %up.1.after_ref), calls=%async_computation | async-start | bytes 262144 | tf_op jit(solution)/shard_map/all_to_all | solution.py:301
  19.3 0.0 copy-done
  19.3 0.0 copy-start.1
  19.3 0.0 copy-start.5
  19.4 3.3 %collective-permute-start.1 = (bf16[2,128,256]{2,1,0:T(8,128)(2,1)S(1)}, bf16[2,128,256]{2,1,0:T(8,128)(2,1)S(1)}, u32[]{:S(2)}, u32[]{:S(2)}) collective-permute-start(bf16[2,128,256]{2,1,0:T(8,128)(2,1)S(1)} %get-tuple-element.10.after_ref), channel_id=1, source_target_pairs={{16,0},{32,16},{48,32},{64,48},{80,64},{96,80},{112,96},{128,112},... | collective-permute-start | bytes 393224 | tf_op jit(solution)/shard_map/ppermute | solution.py:288
  22.7 3.1 %collective-permute-start = (bf16[2,128,256]{2,1,0:T(8,128)(2,1)S(1)}, bf16[2,128,256]{2,1,0:T(8,128)(2,1)S(1)}, u32[]{:S(2)}, u32[]{:S(2)}) collective-permute-start(bf16[2,128,256]{2,1,0:T(8,128)(2,1)S(1)} %get-tuple-element.9), channel_id=1, source_target_pairs={{0,16},{16,32},{32,48},{48,64},{64,80},{80,96},{96,112},{112,128},... | collective-permute-start | bytes 393224 | tf_op jit(solution)/shard_map/ppermute | solution.py:287
  25.8 0.0 copy-done.1
  25.8 0.0 copy-done.5
  25.8 1.2 %weights.1.after_ref.weights_ref = bf16[256,1024]{1,0:T(8,128)(2,1)S(1)} custom-call(s32[16]{0:T(128)S(1)} %bitcast.15, f32[16,64,64]{2,1,0:T(8,128)S(1)} %bitcast.11, bf16[2,128,256]{2,1,0:T(8,128)(2,1)S(1)} %get-tuple-element.10.after_ref), custom_call_target="tpu_custom_call" | custom-call | flops 100000000 | bytes 1048576 | tf_op jit(solution)/shard_map/weights/pallas_call | solution.py:213
  27.0 0.6 %all-to-all-done.in_ref = bf16[16,32,128]{2,1,0:T(8,128)(2,1)S(1)} async-done(((bf16[16,32,128]{2,1,0:T(8,128)(2,1)}), bf16[16,32,128]{2,1,0:T(8,128)(2,1)S(1)}, u32[]{:S(2)}, u32[]{:S(2)}) %all-to-all-start) | async-done | bytes 131104 | tf_op jit(solution)/shard_map/all_to_all | solution.py:301
  27.6 0.7 %sum.1.after_sum_ref = bf16[32,32,128]{2,1,0:T(8,128)(2,1)} custom-call(bf16[16,32,128]{2,1,0:T(8,128)(2,1)S(1)} %all-to-all-done.in_ref, bf16[256,1024]{1,0:T(8,128)(2,1)S(1)} %weights.1.after_ref.weights_ref), custom_call_target="tpu_custom_call" | custom-call | flops 30000001024 | bytes 524288 | tf_op jit(solution)/shard_map/sum/pallas_call | solution.py:213
  28.4 10.2 %all-to-all-start.1 = ((bf16[32,32,128]{2,1,0:T(8,128)(2,1)}), bf16[32,32,128]{2,1,0:T(8,128)(2,1)S(1)}, u32[]{:S(2)}, u32[]{:S(2)}) async-start(bf16[32,32,128]{2,1,0:T(8,128)(2,1)} %sum.1.after_sum_ref), calls=%async_computation.1 | async-start | bytes 524288 | tf_op jit(solution)/shard_map/all_to_all | solution.py:316
  38.5 0.0 collective-permute-done.1.after_ref
  38.6 0.0 collective-permute-done.before_ref
  38.6 0.1 rim.1
  38.6 2.0 %collective-permute-start.2 = (bf16[6,128,256]{2,1,0:T(8,128)(2,1)S(1)}, bf16[6,128,256]{2,1,0:T(8,128)(2,1)S(1)}, u32[]{:S(2)}, u32[]{:S(2)}) collective-permute-start(bf16[6,128,256]{2,1,0:T(8,128)(2,1)S(1)} %get-tuple-element.11), channel_id=1, source_target_pairs={{0,1},{1,2},{2,3},{3,4},{4,5},{5,6},{6,7},{7,8},{8,9},{9,10},{10,1... | collective-permute-start | bytes 1179656 | tf_op jit(solution)/shard_map/ppermute | solution.py:317
  40.6 0.0 copy-start.6
  40.6 1.3 %collective-permute-start.3 = (bf16[6,128,256]{2,1,0:T(8,128)(2,1)S(1)}, bf16[6,128,256]{2,1,0:T(8,128)(2,1)S(1)}, u32[]{:S(2)}, u32[]{:S(2)}) collective-permute-start(bf16[6,128,256]{2,1,0:T(8,128)(2,1)S(1)} %get-tuple-element.12), channel_id=1, source_target_pairs={{1,0},{2,1},{3,2},{4,3},{5,4},{6,5},{7,6},{8,7},{9,8},{10,9},{11,1... | collective-permute-start | bytes 1179656 | tf_op jit(solution)/shard_map/ppermute | solution.py:318
  41.9 1.8 %all-to-all-done.1.tops_ref = bf16[32,32,128]{2,1,0:T(8,128)(2,1)S(1)} async-done(((bf16[32,32,128]{2,1,0:T(8,128)(2,1)}), bf16[32,32,128]{2,1,0:T(8,128)(2,1)S(1)}, u32[]{:S(2)}, u32[]{:S(2)}) %all-to-all-start.1) | async-done | bytes 262176 | tf_op jit(solution)/shard_map/all_to_all | solution.py:316
  43.7 1.0 %couple.1.after_ref = bf16[4,32,128]{2,1,0:T(8,128)(2,1)} custom-call(bf16[32,32,128]{2,1,0:T(8,128)(2,1)S(1)} %all-to-all-done.1.tops_ref, bf16[256,1024]{1,0:T(8,128)(2,1)S(1)} %weights.1.after_ref.weights_ref), custom_call_target="tpu_custom_call" | custom-call | flops 30000001024 | bytes 524288 | tf_op jit(solution)/shard_map/couple/pallas_call | solution.py:213
  44.7 4.8 %all-to-all-start.2 = ((bf16[4,32,128]{2,1,0:T(8,128)(2,1)}), bf16[4,32,128]{2,1,0:T(8,128)(2,1)S(1)}, u32[]{:S(2)}, u32[]{:S(2)}) async-start(bf16[4,32,128]{2,1,0:T(8,128)(2,1)} %couple.1.after_ref), calls=%async_computation.2 | async-start | bytes 65536 | tf_op jit(solution)/shard_map/all_to_all | solution.py:353
  49.5 0.0 copy-done.6
  49.5 0.1 reshape.21.lists_ref
  49.6 0.0 copy-start.2
  49.6 0.0 copy-start.3
  49.6 0.0 copy-start.4
  49.6 1.5 %hold.1.blocks_ref = bf16[4,2,6,128,128]{4,3,2,1,0:T(8,128)(2,1)S(1)} custom-call(bf16[4,2,6,128,128]{4,3,2,1,0:T(8,128)(2,1)} %blocks_ref.1, bf16[4,32,128]{2,1,0:T(8,128)(2,1)} %couple.1.after_ref), custom_call_target="tpu_custom_call" | custom-call | flops 1000000 | bytes 2097152 | tf_op jit(solution)/shard_map/hold/pallas_call | solution.py:213
  51.1 0.0 copy-done.2
  51.1 0.0 copy-done.3
  51.1 0.0 copy-done.4
  51.1 1.3 %far.1.far_ref = bf16[1024,128]{1,0:T(8,128)(2,1)S(1)} custom-call(f32[4,2,64,64]{3,2,1,0:T(8,128)S(1)} %bitcast.12, f32[8,64,64]{2,1,0:T(8,128)S(1)} %bitcast.13, bf16[8,64,128]{2,1,0:T(8,128)(2,1)S(1)} %bitcast.14, bf16[4,32,128]{2,1,0:T(8,128)(2,1)} %couple.1.after_ref), custom_call_target="tpu_custom_call" | custom-call | flops 100000000 | bytes 1048576 | tf_op jit(solution)/shard_map/far/pallas_call | solution.py:213
  52.4 0.0 collective-permute-done.2.left_ref
  52.4 0.0 collective-permute-done.3.right_ref
  52.4 1.3 %near.1.near_ref = f32[8,128,256]{2,1,0:T(8,128)S(1)} custom-call(s32[48]{0:T(128)S(1)} %reshape.21.lists_ref, bf16[4,2,128,256]{3,2,1,0:T(8,128)(2,1)S(1)} %copy-done, bf16[2,128,256]{2,1,0:T(8,128)(2,1)S(1)} %collective-permute-done.before_ref, bf16[2,128,256]{2,1,0:T(8,128)(2,1)S(1)} %collective-permute-done.1.after_ref, ...), custom_call_target="tpu_custom_call" | custom-call | flops 402653184 | bytes 4194304 | tf_op jit(solution)/shard_map/near/pallas_call | solution.py:213
  53.7 0.2 all-to-all-done.2.coeff_ref
  53.9 1.1 %final.1 = bf16[8,128,256]{2,1,0:T(8,128)(2,1)} custom-call(f32[8,128,256]{2,1,0:T(8,128)S(1)} %near.1.near_ref, bf16[1024,128]{1,0:T(8,128)(2,1)S(1)} %far.1.far_ref, bf16[4,32,128]{2,1,0:T(8,128)(2,1)S(1)} %all-to-all-done.2.coeff_ref), custom_call_target="tpu_custom_call" | custom-call | flops 67108864 | bytes 2097152 | tf_op jit(solution)/shard_map/final/pallas_call | solution.py:213
  (1 shorter events, 0.0 us)
Async XLA Ops:
  0.0 19.3 %copy-start = (bf16[4,2,128,256]{3,2,1,0:T(8,128)(2,1)S(1)}, bf16[4,2,128,256]{3,2,1,0:T(8,128)(2,1)}, u32[]{:S(2)}) copy-start(bf16[4,2,128,256]{3,2,1,0:T(8,128)(2,1)} %slip_ref.5) | copy-start | bytes 1572868
  2.9 24.7 %all-to-all-start = ((bf16[16,32,128]{2,1,0:T(8,128)(2,1)}), bf16[16,32,128]{2,1,0:T(8,128)(2,1)S(1)}, u32[]{:S(2)}, u32[]{:S(2)}) async-start(bf16[16,32,128]{2,1,0:T(8,128)(2,1)} %up.1.after_ref), calls=%async_computation | async-start | bytes 262144 | tf_op jit(solution)/shard_map/all_to_all | solution.py:301
  19.3 6.4 %copy-start.1 = (f32[1,16,64,64]{3,2,1,0:T(8,128)S(1)}, f32[1,16,64,64]{3,2,1,0:T(8,128)}, u32[]{:S(2)}) copy-start(f32[1,16,64,64]{3,2,1,0:T(8,128)} %param.21) | copy-start | bytes 786436
  19.3 6.4 %copy-start.5 = (s32[1,16]{1,0:T(1,128)S(1)}, s32[1,16]{1,0:T(1,128)}, u32[]{:S(2)}) copy-start(s32[1,16]{1,0:T(1,128)} %param.20) | copy-start | bytes 196
  19.4 19.2 %collective-permute-start.1 = (bf16[2,128,256]{2,1,0:T(8,128)(2,1)S(1)}, bf16[2,128,256]{2,1,0:T(8,128)(2,1)S(1)}, u32[]{:S(2)}, u32[]{:S(2)}) collective-permute-start(bf16[2,128,256]{2,1,0:T(8,128)(2,1)S(1)} %get-tuple-element.10.after_ref), channel_id=1, source_target_pairs={{16,0},{32,16},{48,32},{64,48},{80,64},{96,80},{112,96},{128,112},... | collective-permute-start | bytes 393224 | tf_op jit(solution)/shard_map/ppermute | solution.py:288
  22.7 15.9 %collective-permute-start = (bf16[2,128,256]{2,1,0:T(8,128)(2,1)S(1)}, bf16[2,128,256]{2,1,0:T(8,128)(2,1)S(1)}, u32[]{:S(2)}, u32[]{:S(2)}) collective-permute-start(bf16[2,128,256]{2,1,0:T(8,128)(2,1)S(1)} %get-tuple-element.9), channel_id=1, source_target_pairs={{0,16},{16,32},{32,48},{48,64},{64,80},{80,96},{96,112},{112,128},... | collective-permute-start | bytes 393224 | tf_op jit(solution)/shard_map/ppermute | solution.py:287
  28.4 15.4 %all-to-all-start.1 = ((bf16[32,32,128]{2,1,0:T(8,128)(2,1)}), bf16[32,32,128]{2,1,0:T(8,128)(2,1)S(1)}, u32[]{:S(2)}, u32[]{:S(2)}) async-start(bf16[32,32,128]{2,1,0:T(8,128)(2,1)} %sum.1.after_sum_ref), calls=%async_computation.1 | async-start | bytes 524288 | tf_op jit(solution)/shard_map/all_to_all | solution.py:316
  38.6 13.8 %collective-permute-start.2 = (bf16[6,128,256]{2,1,0:T(8,128)(2,1)S(1)}, bf16[6,128,256]{2,1,0:T(8,128)(2,1)S(1)}, u32[]{:S(2)}, u32[]{:S(2)}) collective-permute-start(bf16[6,128,256]{2,1,0:T(8,128)(2,1)S(1)} %get-tuple-element.11), channel_id=1, source_target_pairs={{0,1},{1,2},{2,3},{3,4},{4,5},{5,6},{6,7},{7,8},{8,9},{9,10},{10,1... | collective-permute-start | bytes 1179656 | tf_op jit(solution)/shard_map/ppermute | solution.py:317
  40.6 8.9 %copy-start.6 = (s32[4,2,6]{2,1,0:T(2,128)S(1)}, s32[4,2,6]{2,1,0:T(2,128)}, u32[]{:S(2)}) copy-start(s32[4,2,6]{2,1,0:T(2,128)} %param.12) | copy-start | bytes 580
  40.6 11.8 %collective-permute-start.3 = (bf16[6,128,256]{2,1,0:T(8,128)(2,1)S(1)}, bf16[6,128,256]{2,1,0:T(8,128)(2,1)S(1)}, u32[]{:S(2)}, u32[]{:S(2)}) collective-permute-start(bf16[6,128,256]{2,1,0:T(8,128)(2,1)S(1)} %get-tuple-element.12), channel_id=1, source_target_pairs={{1,0},{2,1},{3,2},{4,3},{5,4},{6,5},{7,6},{8,7},{9,8},{10,9},{11,1... | collective-permute-start | bytes 1179656 | tf_op jit(solution)/shard_map/ppermute | solution.py:318
  44.7 9.2 %all-to-all-start.2 = ((bf16[4,32,128]{2,1,0:T(8,128)(2,1)}), bf16[4,32,128]{2,1,0:T(8,128)(2,1)S(1)}, u32[]{:S(2)}, u32[]{:S(2)}) async-start(bf16[4,32,128]{2,1,0:T(8,128)(2,1)} %couple.1.after_ref), calls=%async_computation.2 | async-start | bytes 65536 | tf_op jit(solution)/shard_map/all_to_all | solution.py:353
  49.6 1.5 %copy-start.2 = (f32[1,4,2,64,64]{4,3,2,1,0:T(8,128)S(1)}, f32[1,4,2,64,64]{4,3,2,1,0:T(8,128)}, u32[]{:S(2)}) copy-start(f32[1,4,2,64,64]{4,3,2,1,0:T(8,128)} %param.19) | copy-start | bytes 393220
  49.6 1.5 %copy-start.3 = (f32[4,2,64,64]{3,2,1,0:T(8,128)S(1)}, f32[4,2,64,64]{3,2,1,0:T(8,128)}, u32[]{:S(2)}) copy-start(f32[4,2,64,64]{3,2,1,0:T(8,128)} %param.17) | copy-start | bytes 393220
  49.6 1.5 %copy-start.4 = (bf16[4,2,64,128]{3,2,1,0:T(8,128)(2,1)S(1)}, bf16[4,2,64,128]{3,2,1,0:T(8,128)(2,1)}, u32[]{:S(2)}) copy-start(bf16[4,2,64,128]{3,2,1,0:T(8,128)(2,1)} %param.15) | copy-start | bytes 393220
